TPU v7x, 32 devices: a whole 2x2x4 slice. The times are simulated.
32 devices in a mesh: fsdp: 32 (over z, y, x, core).
Axes of the slice: x: 2, y: 2, z: 4, core: 2. Of those that a mesh axis runs over, the one named last changes fastest.
Arguments:
- inputs: bfloat16 [32, 128, 960], P('fsdp'), may hold values from -6 to 6
- out_cotangent: bfloat16 [32, 128, 960], P('fsdp'), may hold values from -6 to 6
- attn_gain: float32 [960], replicated, may hold values from 0.5 to 1.5
- mlp_gain: float32 [960], replicated, may hold values from 0.5 to 1.5
- query_weight: bfloat16 [921600], P('fsdp'), may hold values from -0.1875 to 0.1875
- key_matrix: bfloat16 [307200], P('fsdp'), may hold values from -0.1875 to 0.1875
- value_matrix: bfloat16 [307200], P('fsdp'), may hold values from -0.1875 to 0.1875
- output_weight: bfloat16 [921600], P('fsdp'), may hold values from -0.5 to 0.5
- gate_weight: bfloat16 [2457600], P('fsdp'), may hold values from -0.1875 to 0.1875
- up_weight: bfloat16 [2457600], P('fsdp'), may hold values from -0.1875 to 0.1875
- down_weight: bfloat16 [2457600], P('fsdp'), may hold values from -0.125 to 0.125
Outputs:
- output: bfloat16 [32, 128, 960], P('fsdp')
- input_grad: float32 [32, 128, 960], P('fsdp')
- query_grad: float32 [921600], P('fsdp')
- key_grad: float32 [307200], P('fsdp')
- value_grad: float32 [307200], P('fsdp')
- output_grad: float32 [921600], P('fsdp')
- gate_grad: float32 [2457600], P('fsdp')
- up_grad: float32 [2457600], P('fsdp')
- down_grad: float32 [2457600], P('fsdp')
- attn_gain_grad: float32 [960], replicated
- mlp_gain_grad: float32 [960], replicated
All inputs are finite; a program needn't handle non-finite values.
Results may differ from a plain program's by a relative error of at most 0.015.
Values may be sent and summed in bfloat16 or wider, within the bound.
A program may use at most 192 MiB of HBM per device.

v0:
```python
import jax
import jax.numpy as jnp
from jax import lax
from jax.sharding import PartitionSpec as P

QUERY_HEADS = 15
KEY_VALUE_HEADS = 5
HEAD_DIMENSION = 64
FEEDFORWARD_SIZE = 2560


EPS = 1e-05
THETA = 100000.0
MASKED = -1e30


def rope_tables(sequence_length, half_width):
    position = jnp.arange(sequence_length).astype(jnp.float32)
    freqs = THETA ** (-(jnp.arange(half_width).astype(jnp.float32) * 2.0) / (2.0 * half_width))
    angle = position[:, None] * freqs[None, :]
    return (jnp.cos(angle)[:, None, :], jnp.sin(angle)[:, None, :])


def apply_rotary(tensor, cosine_lookup, sine_lookup, rotation_sign):
    half_width = tensor.shape[-1] // 2
    first = tensor[..., :half_width]
    second = tensor[..., half_width:]
    return jnp.concatenate(
        [
            first * cosine_lookup - rotation_sign * second * sine_lookup,
            rotation_sign * first * sine_lookup + second * cosine_lookup,
        ],
        axis=-1,
    )


def norm_forward(value_rows, gain):
    scale = lax.rsqrt(jnp.mean(value_rows * value_rows, axis=-1, keepdims=True) + EPS)
    unit = value_rows * scale
    return (unit, scale, (unit * gain).astype(jnp.bfloat16))


def norm_backward(d_normed, unit, scale, gain):
    d_unit = d_normed * gain
    d_input = scale * (d_unit - unit * jnp.mean(d_unit * unit, axis=-1, keepdims=True))
    return (d_input, jnp.sum(d_normed * unit, axis=0))


def matrix_product(left, right):
    return jnp.dot(left, right, preferred_element_type=jnp.float32)


def back_product(left, right):
    return jnp.einsum("tf,df->td", left, right, preferred_element_type=jnp.float32)


def masked_scores(query_rows, key_rows, causal, factor):
    raw = (
        jnp.einsum("bqngd,bknd->bngqk", query_rows, key_rows, preferred_element_type=jnp.float32)
        * factor
    )
    return jnp.where(causal[None, None, None], raw, MASKED)


def flat_slice(left, right, count, stretch):
    product = jnp.einsum("tr,tf->rf", left, right, preferred_element_type=jnp.float32).reshape(-1)
    return product.reshape(count, stretch)


def gradient_term(pairs, devices, count):
    return jnp.concatenate(
        [
            flat_slice(left, right, count, left.shape[1] * right.shape[1] // devices)
            for left, right in pairs
        ],
        axis=1,
    )


def split_shards(joined, pairs, devices):
    pieces = []
    offset = 0
    for left, right in pairs:
        stretch = left.shape[1] * right.shape[1] // devices
        pieces.append(joined[0, offset : offset + stretch])
        offset = offset + stretch
    return pieces


def body(
    inputs,
    out_cotangent,
    attn_gain,
    mlp_gain,
    query_weight,
    key_matrix,
    value_matrix,
    output_weight,
    gate_weight,
    up_weight,
    down_weight,
):
    batch_count, sequence_length, model_width = inputs.shape
    row_count = batch_count * sequence_length
    devices = lax.axis_size("fsdp")
    group_count = QUERY_HEADS // KEY_VALUE_HEADS
    q_width = QUERY_HEADS * HEAD_DIMENSION
    key_value_width = KEY_VALUE_HEADS * HEAD_DIMENSION
    factor = HEAD_DIMENSION ** (-0.5)
    cosine_lookup, sine_lookup = rope_tables(sequence_length, HEAD_DIMENSION // 2)
    causal = jnp.arange(sequence_length)[:, None] >= jnp.arange(sequence_length)[None, :]
    full_query, full_key, full_value, full_output = (
        lax.all_gather(query_weight, "fsdp", axis=0, tiled=True),
        lax.all_gather(key_matrix, "fsdp", axis=0, tiled=True),
        lax.all_gather(value_matrix, "fsdp", axis=0, tiled=True),
        lax.all_gather(output_weight, "fsdp", axis=0, tiled=True),
    )
    w_query = full_query.reshape(model_width, q_width)
    key_projection_full = full_key.reshape(model_width, key_value_width)
    value_projection_full = full_value.reshape(model_width, key_value_width)
    w_output = full_output.reshape(q_width, model_width)
    inputs_f32 = inputs.reshape(row_count, model_width).astype(jnp.float32)
    unit_one, scale_one, first_normalized = norm_forward(inputs_f32, attn_gain)
    query_rows = apply_rotary(
        matrix_product(first_normalized, w_query).reshape(
            batch_count, sequence_length, QUERY_HEADS, HEAD_DIMENSION
        ),
        cosine_lookup,
        sine_lookup,
        1.0,
    )
    query_rows = query_rows.astype(jnp.bfloat16).reshape(
        batch_count, sequence_length, KEY_VALUE_HEADS, group_count, HEAD_DIMENSION
    )
    key_rows = apply_rotary(
        matrix_product(first_normalized, key_projection_full).reshape(
            batch_count, sequence_length, KEY_VALUE_HEADS, HEAD_DIMENSION
        ),
        cosine_lookup,
        sine_lookup,
        1.0,
    )
    key_rows = key_rows.astype(jnp.bfloat16)
    value_rows = (
        matrix_product(first_normalized, value_projection_full)
        .astype(jnp.bfloat16)
        .reshape(batch_count, sequence_length, KEY_VALUE_HEADS, HEAD_DIMENSION)
    )
    scores = masked_scores(query_rows, key_rows, causal, factor)
    row_top = jnp.max(scores, axis=-1, keepdims=True)
    log_total = row_top + jnp.log(jnp.sum(jnp.exp(scores - row_top), axis=-1, keepdims=True))
    probs = jnp.exp(scores - log_total).astype(jnp.bfloat16)
    attended = jnp.einsum(
        "bngqk,bknd->bqngd", probs, value_rows, preferred_element_type=jnp.float32
    )
    attended = attended.astype(jnp.bfloat16).reshape(row_count, q_width)
    hidden = inputs_f32 + matrix_product(attended, w_output)
    full_gate, full_up, full_down = (
        lax.all_gather(gate_weight, "fsdp", axis=0, tiled=True),
        lax.all_gather(up_weight, "fsdp", axis=0, tiled=True),
        lax.all_gather(down_weight, "fsdp", axis=0, tiled=True),
    )
    w_gate = full_gate.reshape(model_width, FEEDFORWARD_SIZE)
    w_up = full_up.reshape(model_width, FEEDFORWARD_SIZE)
    w_down = full_down.reshape(FEEDFORWARD_SIZE, model_width)
    unit_two, scale_two, normed_two = norm_forward(hidden, mlp_gain)
    gate = matrix_product(normed_two, w_gate)
    up_val = matrix_product(normed_two, w_up)
    sigmoid_gate = jax.nn.sigmoid(gate)
    activated = gate * sigmoid_gate
    mixed = (activated * up_val).astype(jnp.bfloat16)
    output = (
        (hidden + matrix_product(mixed, w_down))
        .astype(jnp.bfloat16)
        .reshape(batch_count, sequence_length, model_width)
    )
    again_gate, again_up, again_down = (
        lax.all_gather(gate_weight, "fsdp", axis=0, tiled=True),
        lax.all_gather(up_weight, "fsdp", axis=0, tiled=True),
        lax.all_gather(down_weight, "fsdp", axis=0, tiled=True),
    )
    w_gate = again_gate.reshape(model_width, FEEDFORWARD_SIZE)
    w_up = again_up.reshape(model_width, FEEDFORWARD_SIZE)
    w_down = again_down.reshape(FEEDFORWARD_SIZE, model_width)
    cotangent = out_cotangent.reshape(row_count, model_width)
    d_mixed = back_product(cotangent, w_down)
    d_gate = (d_mixed * up_val * (sigmoid_gate * (1.0 + gate * (1.0 - sigmoid_gate)))).astype(
        jnp.bfloat16
    )
    d_up = (d_mixed * activated).astype(jnp.bfloat16)
    mlp_pairs = [(normed_two, d_gate), (normed_two, d_up), (mixed, cotangent)]
    mlp_joined = lax.psum_scatter(
        gradient_term(mlp_pairs, devices, lax.axis_size("fsdp") * 1),
        "fsdp",
        scatter_dimension=0,
        tiled=True,
    )
    mlp_shards = split_shards(mlp_joined, mlp_pairs, devices)
    d_normed_two = back_product(d_gate, w_gate) + back_product(d_up, w_up)
    d_hid_norm, d_mlp_gain = norm_backward(d_normed_two, unit_two, scale_two, mlp_gain)
    d_hidden = cotangent.astype(jnp.float32) + d_hid_norm
    d_branch = d_hidden.astype(jnp.bfloat16)
    again_query, again_key, again_value, again_output = (
        lax.all_gather(query_weight, "fsdp", axis=0, tiled=True),
        lax.all_gather(key_matrix, "fsdp", axis=0, tiled=True),
        lax.all_gather(value_matrix, "fsdp", axis=0, tiled=True),
        lax.all_gather(output_weight, "fsdp", axis=0, tiled=True),
    )
    w_query = again_query.reshape(model_width, q_width)
    key_projection_full = again_key.reshape(model_width, key_value_width)
    value_projection_full = again_value.reshape(model_width, key_value_width)
    w_output = again_output.reshape(q_width, model_width)
    attended_gradient = back_product(d_branch, w_output).astype(jnp.bfloat16)
    attended_gradient = attended_gradient.reshape(
        batch_count, sequence_length, KEY_VALUE_HEADS, group_count, HEAD_DIMENSION
    )
    scores_again = masked_scores(query_rows, key_rows, causal, factor)
    probs_again = jnp.exp(scores_again - log_total).astype(jnp.bfloat16)
    d_probs = jnp.einsum(
        "bqngd,bknd->bngqk", attended_gradient, value_rows, preferred_element_type=jnp.float32
    )
    value_rows_gradient = jnp.einsum(
        "bngqk,bqngd->bknd", probs_again, attended_gradient, preferred_element_type=jnp.float32
    )
    probs_f32 = probs_again.astype(jnp.float32)
    delta = jnp.sum(probs_f32 * d_probs, axis=-1, keepdims=True)
    d_scores = (probs_f32 * (d_probs - delta) * factor).astype(jnp.bfloat16)
    d_queries = jnp.einsum(
        "bngqk,bknd->bqngd", d_scores, key_rows, preferred_element_type=jnp.float32
    )
    key_rows_gradient = jnp.einsum(
        "bngqk,bqngd->bknd", d_scores, query_rows, preferred_element_type=jnp.float32
    )
    d_queries = d_queries.reshape(batch_count, sequence_length, QUERY_HEADS, HEAD_DIMENSION)
    d_query_in = (
        apply_rotary(d_queries, cosine_lookup, sine_lookup, -1.0)
        .reshape(row_count, q_width)
        .astype(jnp.bfloat16)
    )
    key_input_gradient = (
        apply_rotary(key_rows_gradient, cosine_lookup, sine_lookup, -1.0)
        .reshape(row_count, key_value_width)
        .astype(jnp.bfloat16)
    )
    value_input_gradient = value_rows_gradient.reshape(row_count, key_value_width).astype(
        jnp.bfloat16
    )
    d_normed_one = (
        back_product(d_query_in, w_query)
        + back_product(key_input_gradient, key_projection_full)
        + back_product(value_input_gradient, value_projection_full)
    )
    d_in_norm, d_attn_gain = norm_backward(d_normed_one, unit_one, scale_one, attn_gain)
    input_grad = (d_hidden + d_in_norm).reshape(batch_count, sequence_length, model_width)
    attn_pairs = [
        (first_normalized, d_query_in),
        (first_normalized, key_input_gradient),
        (first_normalized, value_input_gradient),
        (attended, d_branch),
    ]
    attn_joined = lax.psum_scatter(
        gradient_term(attn_pairs, devices, lax.axis_size("fsdp") * 1),
        "fsdp",
        scatter_dimension=0,
        tiled=True,
    )
    shards = split_shards(attn_joined, attn_pairs, devices) + mlp_shards
    gain_sums = lax.psum((d_attn_gain, d_mlp_gain), "fsdp")
    return (
        output,
        input_grad,
        shards[0],
        shards[1],
        shards[2],
        shards[3],
        shards[4],
        shards[5],
        shards[6],
        gain_sums[0],
        gain_sums[1],
    )


def solution(mesh):
    in_specs = (
        P("fsdp", None, None),
        P("fsdp", None, None),
        P(),
        P(),
        P("fsdp"),
        P("fsdp"),
        P("fsdp"),
        P("fsdp"),
        P("fsdp"),
        P("fsdp"),
        P("fsdp"),
    )
    out_specs = (
        P("fsdp", None, None),
        P("fsdp", None, None),
        P("fsdp"),
        P("fsdp"),
        P("fsdp"),
        P("fsdp"),
        P("fsdp"),
        P("fsdp"),
        P("fsdp"),
        P(),
        P(),
    )
    return jax.shard_map(body, mesh=mesh, in_specs=in_specs, out_specs=out_specs, check_vma=False)
```

profile of v0, /device:TPU:0, one launch (start us, length us, event | category | flops | bytes accessed | tf_op | source)
XLA Modules:
  0.0 1057.8 jit_solution(11637208474495817106)
XLA Ops:
  7.2 1.5 reshape.456
  8.8 1.5 reshape.458
  10.4 0.7 all-gather.10.cloned.1.call-update
  11.2 0.5 all-gather.12.cloned.1.call-update
  11.8 0.5 all-gather.14.cloned.1.call-update
  12.3 0.8 reshape.452
  13.1 47.7 %all-gather = bf16[32,1,9600]{2,1,0:T(2,128)(2,1)S(1)} all-gather(bf16[1,1,9600]{2,1,0:T(2,128)(2,1)S(1)} %reshape.452), channel_id=1, replica_groups=mesh['fsdp'=32] {'fsdp'}, dimensions={0}, use_global_device_ids=true | all-gather | bytes 633600 | tf_op jit(solution)/shard_map/all_gather | solution.py:115
  60.8 3.7 reduce.3
  64.5 0.8 reshape.435
  65.3 42.4 %all-gather.1 = bf16[32,1,9600]{2,1,0:T(2,128)(2,1)S(1)} all-gather(bf16[1,1,9600]{2,1,0:T(2,128)(2,1)S(1)} %reshape.454), channel_id=1, replica_groups=mesh['fsdp'=32] {'fsdp'}, dimensions={0}, use_global_device_ids=true | all-gather | bytes 633600 | tf_op jit(solution)/shard_map/all_gather | solution.py:114
  107.7 3.7 reduce.4
  111.4 0.8 reshape.437
  112.7 0.5 convolution_bitcast_fusion.4
  113.1 0.7 broadcast_multiply_fusion
  113.9 0.6 convolution_convert_fusion.2
  114.6 40.9 %reduce.5 = bf16[32,28800]{1,0:T(8,128)(2,1)} reduce(bf16[32,1,28800]{2,1,0:T(2,128)(2,1)} %all-gather.16.cloned.1.call-done, bf16[]{:T(256)} %constant.36), dimensions={1}, to_apply=%all-gather.2.reduce_sub_computation | reduce | bytes 3686402 | tf_op jit(solution)/shard_map/all_gather | solution.py:113
  155.6 3.0 reshape.438
  158.6 2.5 copy.36
  161.0 40.8 %reduce.6 = bf16[32,28800]{1,0:T(8,128)(2,1)} reduce(bf16[32,1,28800]{2,1,0:T(2,128)(2,1)} %all-gather.18.cloned.1.call-done, bf16[]{:T(256)} %constant.36), dimensions={1}, to_apply=%all-gather.3.reduce_sub_computation | reduce | bytes 3686402 | tf_op jit(solution)/shard_map/all_gather | solution.py:116
  201.9 4.1 reshape.441
  206.0 2.5 convolution_bitcast_fusion.1
  210.2 0.9 multiply_reduce_fusion.2
  211.3 10.1 reshape.442
  221.4 52.0 %all-gather.12.cloned.1.call-done = bf16[2457600]{0:T(1024)(128)(2,1)} async-done(((bf16[76800]{0:T(1024)(128)(2,1)}), bf16[2457600]{0:T(1024)(128)(2,1)}) %all-gather.12.cloned.1.call-update) | async-done | bytes 4915216 | tf_op jit(solution)/shard_map/all_gather | solution.py:160
  273.4 10.0 reshape.443
  283.4 4.5 fusion.57
  288.0 1.9 fusion.58
  289.9 49.5 %all-gather.14.cloned.1.call-done = bf16[2457600]{0:T(1024)(128)(2,1)} async-done(((bf16[76800]{0:T(1024)(128)(2,1)}), bf16[2457600]{0:T(1024)(128)(2,1)}) %all-gather.14.cloned.1.call-update) | async-done | bytes 4915216 | tf_op jit(solution)/shard_map/all_gather | solution.py:161
  339.4 10.0 reshape.444
  349.4 6.4 multiply_convert_fusion
  355.9 1.4 fusion.59
  357.3 4.7 multiply_reduce_fusion
  362.3 0.7 convolution_convert_fusion
  364.7 2.5 fusion.40
  367.2 5.2 fusion.61
  372.4 5.1 fusion.60
  377.5 0.6 subtract_convert_fusion.2
  378.1 0.7 subtract_convert_fusion
  378.8 5.3 reshape_reshape.24
  384.1 1.5 fusion.35
  385.6 3.2 reshape_reshape.23
  388.8 0.8 pad_maximum_fusion.6
  389.6 1.5 fusion.37
  391.1 3.2 reshape_reshape.22
  394.2 0.9 pad_maximum_fusion.3
  395.2 0.7 copy-done.14
  395.9 2.6 fusion.33
  398.4 5.1 reshape_reshape.21
  403.6 6.7 fusion.27
  410.3 10.6 reshape_reshape.27
  420.8 10.3 reshape_reshape.26
  431.2 10.3 reshape_reshape.25
  441.5 20.9 %pad_maximum_fusion = f32[32,230400]{1,0:T(8,128)} fusion(f32[32,76800]{1,0:T(8,128)} %reshape_reshape.27, f32[32,76800]{1,0:T(8,128)} %reshape_reshape.26, f32[32,76800]{1,0:T(8,128)} %reshape_reshape.25), kind=kLoop, calls=%fused_computation | loop fusion | flops 14745600 | bytes 58982400 | tf_op jit(solution)/shard_map/concatenate | solution.py:71
  462.4 6.9 pad_maximum_fusion.1
  469.3 1.5 fusion.63
  470.8 1.5 fusion.62
  472.3 2.4 fusion.20
  474.7 41.7 %all-reduce.2 = (f32[960]{0:T(1024)}, f32[960]{0:T(1024)}) all-reduce(f32[960]{0:T(1024)S(1)} %get-tuple-element.17, f32[960]{0:T(1024)S(1)} %copy-done.34), channel_id=1, replica_groups=mesh['fsdp'=32] {'fsdp'}, use_global_device_ids=true, to_apply=%region_10.11 | all-reduce | flops 1920 | bytes 15360 | tf_op jit(solution)/shard_map/psum | solution.py:268
  516.4 2.0 fusion.19
  518.4 5.4 fusion.5
  523.9 516.7 %all-reduce.6.cloned.1.call-done = (f32[32,76800]{1,0:T(8,128)}, f32[32,230400]{1,0:T(8,128)}) async-done(((f32[32,76800]{1,0:T(8,128)}, f32[32,230400]{1,0:T(8,128)}), (f32[32,76800]{1,0:T(8,128)}, f32[32,230400]{1,0:T(8,128)})) %all-reduce.6.cloned.1.call-update) | async-done | bytes 39321616
  1040.6 2.8 dynamic-slice_reduce_fusion
  1043.4 1.9 dynamic-slice_reduce_fusion.2
  1045.3 5.4 fusion.55
  (114 shorter events, 4.5 us)
Async XLA Ops:
  7.2 58.1 %copy-start.33 = (bf16[9600]{0:T(1024)(128)(2,1)S(1)}, bf16[9600]{0:T(1024)(128)(2,1)}, u32[]{:S(2)}) copy-start(bf16[9600]{0:T(1024)(128)(2,1)} %param.16) | copy-start | bytes 57604
  7.2 107.4 %all-gather.16.cloned.1.call-start = ((), (), s32[]{:S(2)}) async-start(), calls=%async_computation.3 | async-start | bytes 3801600 | tf_op jit(solution)/shard_map/all_gather | solution.py:113
  8.8 152.3 %all-gather.18.cloned.1.call-start = ((), (), s32[]{:S(2)}) async-start(), calls=%async_computation.4 | async-start | bytes 3801600 | tf_op jit(solution)/shard_map/all_gather | solution.py:116
  10.4 200.9 %all-gather.10.cloned.1.call-start = ((), (), s32[]{:S(2)}) async-start(), calls=%async_computation | async-start | bytes 5068800 | tf_op jit(solution)/shard_map/all_gather | solution.py:159
  11.1 262.3 %all-gather.12.cloned.1.call-start = ((), (), s32[]{:S(2)}) async-start(), calls=%async_computation.1 | async-start | bytes 5068800 | tf_op jit(solution)/shard_map/all_gather | solution.py:160
  11.7 327.7 %all-gather.14.cloned.1.call-start = ((), (), s32[]{:S(2)}) async-start(), calls=%async_computation.2 | async-start | bytes 5068800 | tf_op jit(solution)/shard_map/all_gather | solution.py:161
  12.3 1028.3 %all-reduce.6.cloned.1.call-start = ((), (), s32[]{:S(2)}) async-start(), calls=%async_computation.5 | async-start | bytes 78643200
  64.5 48.0 %copy-start.1 = (bf16[1,128,960]{1,2,0:T(8,128)(2,1)S(1)}, bf16[1,128,960]{1,2,0:T(8,128)(2,1)}, u32[]{:S(2)}) copy-start(bf16[1,128,960]{1,2,0:T(8,128)(2,1)} %param.11) | copy-start | bytes 737284
  64.5 48.2 %copy-start.22 = (f32[960]{0:T(1024)S(1)}, f32[960]{0:T(1024)}, u32[]{:S(2)}) copy-start(f32[960]{0:T(1024)} %param.13) | copy-start | bytes 11524
  65.3 49.3 %copy-start.11 = (bf16[960,320]{1,0:T(8,128)(2,1)}, bf16[960,320]{1,0:T(8,128)(2,1)S(1)}, u32[]{:S(2)}) copy-start(bf16[960,320]{1,0:T(8,128)(2,1)S(1)} %reshape.435) | copy-start | bytes 1843204
  112.2 2.4 copy-start.8
  112.7 93.4 %copy-start.31 = (f32[128]{0:T(128)}, f32[128]{0:T(128)S(1)}, u32[]{:S(2)}) copy-start(f32[128]{0:T(128)S(1)} %add_rsqrt_fusion.1) | copy-start | bytes 1540
  113.9 94.7 %copy-start.18 = (f32[128,32]{0,1:T(8,128)}, f32[128,32]{0,1:T(8,128)S(1)}, u32[]{:S(2)}) copy-start(f32[128,32]{0,1:T(8,128)S(1)} %get-tuple-element.39) | copy-start | bytes 49156
  113.9 94.7 %copy-start.23 = (bf16[128,5,32]{0,2,1:T(8,128)(2,1)}, bf16[128,5,32]{0,2,1:T(8,128)(2,1)S(1)}, u32[]{:S(2)}) copy-start(bf16[128,5,32]{0,2,1:T(8,128)(2,1)S(1)} %get-tuple-element.35) | copy-start | bytes 122884
  113.9 94.7 %copy-start.25 = (bf16[128,5,32]{0,2,1:T(8,128)(2,1)}, bf16[128,5,32]{0,2,1:T(8,128)(2,1)S(1)}, u32[]{:S(2)}) copy-start(bf16[128,5,32]{0,2,1:T(8,128)(2,1)S(1)} %get-tuple-element.36) | copy-start | bytes 122884
  114.6 94.8 %copy-start.20 = (bf16[128,320]{0,1:T(8,128)(2,1)}, bf16[128,320]{0,1:T(8,128)(2,1)S(1)}, u32[]{:S(2)}) copy-start(bf16[128,320]{0,1:T(8,128)(2,1)S(1)} %convolution_convert_fusion.2) | copy-start | bytes 245764
  206.0 4.1 copy-start.2
  208.6 1.0 copy-start.16
  208.6 2.5 copy-start.30
  209.0 1.0 copy-start.4
  209.2 0.8 copy-start.28
  209.4 0.8 copy-start.6
  210.2 0.9 copy-start.12
  211.1 10.3 copy-start.35
  211.3 76.7 %copy-start.9 = (bf16[128,960]{0,1:T(8,128)(2,1)}, bf16[128,960]{0,1:T(8,128)(2,1)S(1)}, u32[]{:S(2)}) copy-start(bf16[128,960]{0,1:T(8,128)(2,1)S(1)} %multiply_convert_fusion.3) | copy-start | bytes 737284
  283.4 4.6 copy-start
  339.4 16.4 %slice-start = ((s8[4915200]{0:T(1024)(128)(4,1)}), s8[720896]{0:T(1024)(128)(4,1)S(1)}, s32[]{:S(2)}) async-start(s8[4915200]{0:T(1024)(128)(4,1)} %bitcast.168), calls=%async_computation.6 | async-start | bytes 1441792
  349.4 6.4 slice-start.1
  355.8 1.5 copy-start.36
  357.3 4.7 copy-start.15
  357.3 5.0 copy-start.3
  362.0 1.0 copy-start.7
  362.0 1.4 copy-start.21
  362.0 1.7 copy-start.5
  362.0 1.7 copy-start.29
  362.3 1.8 copy-start.17
  362.3 2.1 copy-start.24
  362.3 2.1 copy-start.26
  363.0 1.7 copy-start.13
  364.0 3.2 copy-start.10
  372.4 5.1 copy-start.19
  372.4 5.1 copy-start.27
  378.8 5.3 copy-start.32
  395.2 0.7 copy-start.14
  469.3 5.4 copy-start.34
Sparse Core Ops, SparseCore 0:
  11.4 67.8 all-gather.15
  82.7 58.4 all-gather.17
  144.2 63.2 all-gather.9
  210.2 63.1 all-gather.11
  276.2 63.1 all-gather.13
  469.4 571.0 all-reduce.5
where the time goes:
time: 1060 us
  waiting for transfers between devices  620 us (58%)
  blocking collectives  132 us (12%)
  other arithmetic  124 us (12%)
  local copies, waits for them, and re-layouts  105 us (10%)
  matrix products  61.9 us (6%)
  between operations  15 us (1%)
    unnamed x7, waiting for transfers between devices  518 us
    all_gather x1, waiting for transfers between devices, body(): lax.all_gather(up_weight, 'fsdp', axis=0, tiled=True)  52 us
    all_gather x1, waiting for transfers between devices, body(): lax.all_gather(down_weight, 'fsdp', axis=0, tiled=True)  49.5 us
    another operation x7, local copies, waits for them, and re-layouts, flat_slice(): return product.reshape(count, stretch)  47.9 us
    all_gather x1, blocking collectives, body(): lax.all_gather(value_matrix, 'fsdp', axis=0, tiled=True)  47.7 us
    all_gather x1, blocking collectives, body(): lax.all_gather(key_matrix, 'fsdp', axis=0, tiled=True)  42.4 us
    psum x1, blocking collectives, body(): gain_sums = lax.psum((d_attn_gain, d_mlp_gain), 'fsdp')  41.7 us
    all_gather x1, other arithmetic, body(): lax.all_gather(query_weight, 'fsdp', axis=0, tiled=True)  40.9 us
  transfers between devices with their start and end apart: 6, of which 3 were waited for; matrix products, arithmetic and copies ran while one was open for 14% of the time, Pallas kernels for 0%

commit v1 on v0

--- a/solution.py
+++ b/solution.py
@@ -1,6 +1,10 @@
+import functools
+
 import jax
 import jax.numpy as jnp
 from jax import lax
+from jax.experimental import pallas as pl
+from jax.experimental.pallas import tpu as pltpu
 from jax.sharding import PartitionSpec as P
 
 QUERY_HEADS = 15
@@ -281,6 +285,472 @@
     )
 
 
+PLANES = 4
+TILE = 16
+
+
+def unit_place(me):
+    return me // 8, (me // 4) % 2, (me // 2) % 2, me % 2
+
+
+def unit_index(z, y, x, c):
+    return ((z * 2 + y) * 2 + x) * 2 + c
+
+
+def partners(me):
+    z, y, x, c = unit_place(me)
+    peers = [unit_index((z + k) % PLANES, y, x, c) for k in range(1, PLANES)]
+    peers.append(unit_index(z, y, 1 - x, c))
+    peers.append(unit_index(z, 1 - y, x, c))
+    peers.append(unit_index(z, y, x, 1 - c))
+    return peers
+
+
+def meet(peers):
+    barrier = pltpu.get_barrier_semaphore()
+    for peer in peers:
+        pl.semaphore_signal(
+            barrier, inc=1, device_id=(peer,), device_id_type=pl.DeviceIdType.MESH
+        )
+    pl.semaphore_wait(barrier, len(peers))
+
+
+def remote(source, target, send, receive, device):
+    return pltpu.make_async_remote_copy(
+        src_ref=source,
+        dst_ref=target,
+        send_sem=send,
+        recv_sem=receive,
+        device_id=(device,),
+        device_id_type=pl.DeviceIdType.MESH,
+    )
+
+
+def gather_kernel(count, *refs):
+    shards, wholes = refs[:count], refs[count : 2 * count]
+    send, receive, local = refs[2 * count :]
+    me = lax.axis_index("fsdp")
+    z, y, x, c = unit_place(me)
+    meet(partners(me))
+
+    def copies(a, phase):
+        whole = wholes[a]
+        x_first = a % 2 == 0
+        if phase == 0:
+            return [
+                remote(
+                    shards[a],
+                    whole.at[z, y, x, c],
+                    send.at[a, k - 1],
+                    receive.at[a, k - 1],
+                    unit_index((z + k) % PLANES, y, x, c),
+                )
+                for k in range(1, PLANES)
+            ]
+        over_x = unit_index(z, y, 1 - x, c)
+        over_y = unit_index(z, 1 - y, x, c)
+        if phase == 1:
+            part, device = whole.at[:, y, x, c], (over_x if x_first else over_y)
+        elif phase == 2:
+            part = whole.at[:, y, :, c] if x_first else whole.at[:, :, x, c]
+            device = over_y if x_first else over_x
+        else:
+            part, device = whole.at[:, :, :, c], unit_index(z, y, x, 1 - c)
+        return [remote(part, part, send.at[a, phase + 2], receive.at[a, phase + 2], device)]
+
+    locals_ = [
+        pltpu.make_async_copy(shards[a], wholes[a].at[z, y, x, c], local.at[a])
+        for a in range(count)
+    ]
+    for a in range(count):
+        for copy in copies(a, 0):
+            copy.start()
+        locals_[a].start()
+    for step in range(count + 3):
+        for phase in (3, 2, 1):
+            a = step - (phase - 1)
+            if 0 <= a < count:
+                if phase == 1:
+                    locals_[a].wait()
+                for copy in copies(a, phase - 1):
+                    copy.wait_recv()
+                for copy in copies(a, phase):
+                    copy.start()
+    for a in range(count):
+        for copy in copies(a, 3):
+            copy.wait_recv()
+        for phase in range(4):
+            for copy in copies(a, phase):
+                copy.wait_send()
+
+
+def gather_blocks(shards, identity):
+    count = len(shards)
+    return pl.pallas_call(
+        functools.partial(gather_kernel, count),
+        out_shape=[jax.ShapeDtypeStruct((PLANES, 2, 2, 2) + s.shape, s.dtype) for s in shards],
+        in_specs=[pl.BlockSpec(memory_space=pl.ANY)] * count,
+        out_specs=[pl.BlockSpec(memory_space=pl.ANY)] * count,
+        scratch_shapes=[
+            pltpu.SemaphoreType.DMA((count, 6)),
+            pltpu.SemaphoreType.DMA((count, 6)),
+            pltpu.SemaphoreType.DMA((count,)),
+        ],
+        compiler_params=pltpu.CompilerParams(collective_id=identity, has_side_effects=True),
+    )(*shards)
+
+
+def scatter_kernel(count, *refs):
+    grads, gain = refs[:count], refs[count]
+    outs, gain_out = refs[count + 1 : 2 * count + 1], refs[2 * count + 1]
+    rest = refs[2 * count + 2 :]
+    held, sibling, second, third, last = (rest[i * count : (i + 1) * count] for i in range(5))
+    gain_a, gain_b, gain_c, gain_z, send, receive, local = rest[5 * count :]
+    me = lax.axis_index("fsdp")
+    z, y, x, c = unit_place(me)
+    meet(partners(me))
+    over_core = unit_index(z, y, x, 1 - c)
+    over_x = unit_index(z, y, 1 - x, c)
+    over_y = unit_index(z, 1 - y, x, c)
+
+    def copies(a, phase):
+        x_first = a % 2 == 0
+        if phase == 0:
+            jobs = [(grads[a].at[:, :, :, 1 - c], sibling[a], over_core)]
+        elif phase == 1:
+            if x_first:
+                jobs = [(held[a].at[:, :, 1 - x], second[a], over_x)]
+            else:
+                jobs = [(held[a].at[:, 1 - y], second[a], over_y)]
+        elif phase == 2:
+            if x_first:
+                jobs = [(held[a].at[:, 1 - y, x], third[a], over_y)]
+            else:
+                jobs = [(held[a].at[:, y, 1 - x], third[a], over_x)]
+        else:
+            jobs = []
+            for k in range(1, PLANES):
+                to = (z + k) % PLANES
+                jobs.append((held[a].at[to, y, x], last[a].at[k - 1], unit_index(to, y, x, c)))
+        return [
+            remote(s, d, send.at[a, phase + i], receive.at[a, phase + i], device)
+            for i, (s, d, device) in enumerate(jobs)
+        ]
+
+    def add(target, term):
+        target[...] = (target[...].astype(jnp.float32) + term[...].astype(jnp.float32)).astype(
+            target.dtype
+        )
+
+    def fold(a, phase):
+        x_first = a % 2 == 0
+        if phase == 0:
+
+            @pl.loop(0, PLANES * 4)
+            def _(i):
+                zz, yy, xx = i // 4, (i // 2) % 2, i % 2
+                add(held[a].at[zz, yy, xx], sibling[a].at[zz, yy, xx])
+
+        elif phase == 1:
+
+            @pl.loop(0, PLANES * 2)
+            def _(i):
+                zz, other = i // 2, i % 2
+                if x_first:
+                    add(held[a].at[zz, other, x], second[a].at[zz, other])
+                else:
+                    add(held[a].at[zz, y, other], second[a].at[zz, other])
+
+        elif phase == 2:
+
+            @pl.loop(0, PLANES)
+            def _(zz):
+                add(held[a].at[zz, y, x], third[a].at[zz])
+
+        else:
+            total = held[a][z, y, x].astype(jnp.float32)
+            for k in range(PLANES - 1):
+                total = total + last[a][k].astype(jnp.float32)
+            outs[a][...] = total
+
+    def gain_copies(phase):
+        if phase < 3:
+            source, target, device = (
+                (gain, gain_a.at[1], over_core),
+                (gain_a.at[0], gain_b.at[1], over_x),
+                (gain_b.at[0], gain_c, over_y),
+            )[phase]
+            jobs = [(source, target, device)]
+        else:
+            jobs = [
+                (gain_z.at[z], gain_z.at[z], unit_index((z + k) % PLANES, y, x, c))
+                for k in range(1, PLANES)
+            ]
+        return [
+            remote(s, d, send.at[count, phase + i], receive.at[count, phase + i], device)
+            for i, (s, d, device) in enumerate(jobs)
+        ]
+
+    def gain_fold(phase):
+        if phase == 0:
+            gain_a[0] = gain[...] + gain_a[1]
+        elif phase == 1:
+            gain_b[0] = gain_a[0] + gain_b[1]
+        elif phase == 2:
+            gain_z[z] = gain_b[0] + gain_c[...]
+        else:
+            gain_out[...] = (gain_z[0] + gain_z[1]) + (gain_z[2] + gain_z[3])
+
+    locals_ = [
+        pltpu.make_async_copy(grads[a].at[:, :, :, c], held[a], local.at[a]) for a in range(count)
+    ]
+    for copy in gain_copies(0):
+        copy.start()
+    for a in range(count):
+        for copy in copies(a, 0):
+            copy.start()
+        locals_[a].start()
+    for step in range(count + 3):
+        for phase in (3, 2, 1, 0):
+            a = step - phase
+            if 0 <= a < count:
+                if phase == 0:
+                    locals_[a].wait()
+                for copy in copies(a, phase):
+                    copy.wait_recv()
+                fold(a, phase)
+                if phase < 3:
+                    for copy in copies(a, phase + 1):
+                        copy.start()
+        if step < 4:
+            for copy in gain_copies(step):
+                copy.wait_recv()
+            gain_fold(step)
+            if step < 3:
+                for copy in gain_copies(step + 1):
+                    copy.start()
+    for phase in range(4):
+        for a in range(count):
+            for copy in copies(a, phase):
+                copy.wait_send()
+        for copy in gain_copies(phase):
+            copy.wait_send()
+
+
+def scatter_blocks(grads, gain, identity):
+    count = len(grads)
+    blocks = [g.shape[4:] for g in grads]
+    kind = grads[0].dtype
+    vmem = pl.BlockSpec(memory_space=pltpu.VMEM)
+
+    def room(lead):
+        return [pltpu.VMEM(lead + b, kind) for b in blocks]
+
+    return pl.pallas_call(
+        functools.partial(scatter_kernel, count),
+        out_shape=[jax.ShapeDtypeStruct(b, jnp.float32) for b in blocks]
+        + [jax.ShapeDtypeStruct(gain.shape, gain.dtype)],
+        in_specs=[pl.BlockSpec(memory_space=pl.ANY)] * count + [vmem],
+        out_specs=[vmem] * (count + 1),
+        scratch_shapes=room((PLANES, 2, 2))
+        + room((PLANES, 2, 2))
+        + room((PLANES, 2))
+        + room((PLANES,))
+        + room((PLANES - 1,))
+        + [
+            pltpu.VMEM((2,) + gain.shape, gain.dtype),
+            pltpu.VMEM((2,) + gain.shape, gain.dtype),
+            pltpu.VMEM(gain.shape, gain.dtype),
+            pltpu.VMEM((PLANES,) + gain.shape, gain.dtype),
+            pltpu.SemaphoreType.DMA((count + 1, 6)),
+            pltpu.SemaphoreType.DMA((count + 1, 6)),
+            pltpu.SemaphoreType.DMA((count,)),
+        ],
+        compiler_params=pltpu.CompilerParams(
+            collective_id=identity, has_side_effects=True, vmem_limit_bytes=48 * 1024 * 1024
+        ),
+    )(*grads, gain)
+
+
+def spread_matrix(width, rows, padded_rows, devices):
+    feature = jnp.arange(width)
+    place = (feature // rows) * padded_rows + feature % rows
+    return (place[:, None] == jnp.arange(devices * padded_rows)[None, :]).astype(jnp.bfloat16)
+
+
+def widen(rows, spread):
+    return matrix_product(rows.astype(jnp.bfloat16), spread).astype(jnp.bfloat16)
+
+
+def narrow_exact(rows, spread):
+    high = lax.reduce_precision(rows, 8, 7)
+    middle = lax.reduce_precision(rows - high, 8, 7)
+    low = rows - high - middle
+    stacked = jnp.concatenate([high, middle, low], axis=0).astype(jnp.bfloat16)
+    stacked = back_product(stacked, spread)
+    count = rows.shape[0]
+    return stacked[:count] + (stacked[count : 2 * count] + stacked[2 * count :])
+
+
+def fast_body(
+    inputs,
+    out_cotangent,
+    attn_gain,
+    mlp_gain,
+    query_weight,
+    key_matrix,
+    value_matrix,
+    output_weight,
+    gate_weight,
+    up_weight,
+    down_weight,
+):
+    _, sequence_length, model_width = inputs.shape
+    tokens = sequence_length
+    devices = lax.axis_size("fsdp")
+    groups = QUERY_HEADS // KEY_VALUE_HEADS
+    q_width = QUERY_HEADS * HEAD_DIMENSION
+    kv_width = KEY_VALUE_HEADS * HEAD_DIMENSION
+    factor = HEAD_DIMENSION ** (-0.5)
+    rows = model_width // devices
+    padded = -(-rows // TILE) * TILE
+    down_rows = FEEDFORWARD_SIZE // devices
+    cosine, sine = rope_tables(sequence_length, HEAD_DIMENSION // 2)
+    causal = jnp.arange(sequence_length)[:, None] >= jnp.arange(sequence_length)[None, :]
+    spread = spread_matrix(model_width, rows, padded, devices)
+
+    def lay(weight):
+        return weight.reshape(rows, -1)
+
+    def fill(matrix):
+        return jnp.pad(matrix, ((0, padded - rows), (0, 0)))
+
+    attn_shard = fill(
+        jnp.concatenate(
+            [lay(query_weight), lay(key_matrix), lay(value_matrix), lay(output_weight)], axis=1
+        )
+    )
+    gathered = gather_blocks(
+        [
+            attn_shard,
+            fill(lay(gate_weight)),
+            fill(lay(up_weight)),
+            down_weight.reshape(down_rows, model_width),
+        ],
+        0,
+    )
+    attn_all, w_gate, w_up, w_down = (g.reshape(-1, g.shape[-1]) for g in gathered)
+    w_qkv = attn_all[:, : q_width + 2 * kv_width]
+    w_output = attn_all[:, q_width + 2 * kv_width :]
+
+    x = inputs.reshape(tokens, model_width).astype(jnp.float32)
+    cotangent = out_cotangent.reshape(tokens, model_width)
+    unit_one, scale_one, normed_one = norm_forward(x, attn_gain)
+    normed_one = widen(normed_one, spread)
+    qkv = matrix_product(normed_one, w_qkv)
+    queries = apply_rotary(
+        qkv[:, :q_width].reshape(tokens, QUERY_HEADS, HEAD_DIMENSION), cosine, sine, 1.0
+    )
+    queries = queries.astype(jnp.bfloat16).reshape(1, tokens, KEY_VALUE_HEADS, groups, HEAD_DIMENSION)
+    keys = apply_rotary(
+        qkv[:, q_width : q_width + kv_width].reshape(tokens, KEY_VALUE_HEADS, HEAD_DIMENSION),
+        cosine,
+        sine,
+        1.0,
+    )
+    keys = keys.astype(jnp.bfloat16)[None]
+    values = (
+        qkv[:, q_width + kv_width :]
+        .astype(jnp.bfloat16)
+        .reshape(1, tokens, KEY_VALUE_HEADS, HEAD_DIMENSION)
+    )
+    scores = masked_scores(queries, keys, causal, factor)
+    row_top = jnp.max(scores, axis=-1, keepdims=True)
+    log_total = row_top + jnp.log(jnp.sum(jnp.exp(scores - row_top), axis=-1, keepdims=True))
+    probs = jnp.exp(scores - log_total).astype(jnp.bfloat16)
+    attended = jnp.einsum("bngqk,bknd->bqngd", probs, values, preferred_element_type=jnp.float32)
+    attended = widen(attended.astype(jnp.bfloat16).reshape(tokens, q_width), spread)
+    hidden = x + matrix_product(attended, w_output)
+    unit_two, scale_two, normed_two = norm_forward(hidden, mlp_gain)
+    normed_two = widen(normed_two, spread)
+    gate = matrix_product(normed_two, w_gate)
+    up_val = matrix_product(normed_two, w_up)
+    sigmoid_gate = jax.nn.sigmoid(gate)
+    activated = gate * sigmoid_gate
+    mixed = (activated * up_val).astype(jnp.bfloat16)
+    output = (hidden + matrix_product(mixed, w_down)).astype(jnp.bfloat16)
+    d_mixed = back_product(cotangent, w_down)
+    d_gate = (d_mixed * up_val * (sigmoid_gate * (1.0 + gate * (1.0 - sigmoid_gate)))).astype(
+        jnp.bfloat16
+    )
+    d_up = (d_mixed * activated).astype(jnp.bfloat16)
+
+    def weight_term(left, right):
+        return jnp.einsum("tr,tf->rf", left, right, preferred_element_type=jnp.float32).astype(
+            jnp.bfloat16
+        )
+
+    gate_term = weight_term(normed_two, d_gate)
+    up_term = weight_term(normed_two, d_up)
+    down_term = weight_term(mixed, cotangent)
+    d_normed_two = narrow_exact(back_product(d_gate, w_gate) + back_product(d_up, w_up), spread)
+    d_hid_norm, d_mlp_gain = norm_backward(d_normed_two, unit_two, scale_two, mlp_gain)
+    d_hidden = cotangent.astype(jnp.float32) + d_hid_norm
+    d_branch = d_hidden.astype(jnp.bfloat16)
+    d_attended = back_product(d_branch, w_output).astype(jnp.bfloat16)
+    d_attended = back_product(d_attended, spread).astype(jnp.bfloat16)
+    d_attended = d_attended.reshape(1, tokens, KEY_VALUE_HEADS, groups, HEAD_DIMENSION)
+    d_probs = jnp.einsum("bqngd,bknd->bngqk", d_attended, values, preferred_element_type=jnp.float32)
+    d_values = jnp.einsum("bngqk,bqngd->bknd", probs, d_attended, preferred_element_type=jnp.float32)
+    probs_f32 = probs.astype(jnp.float32)
+    delta = jnp.sum(probs_f32 * d_probs, axis=-1, keepdims=True)
+    d_scores = (probs_f32 * (d_probs - delta) * factor).astype(jnp.bfloat16)
+    d_queries = jnp.einsum("bngqk,bknd->bqngd", d_scores, keys, preferred_element_type=jnp.float32)
+    d_keys = jnp.einsum("bngqk,bqngd->bknd", d_scores, queries, preferred_element_type=jnp.float32)
+    d_query_in = apply_rotary(
+        d_queries.reshape(tokens, QUERY_HEADS, HEAD_DIMENSION), cosine, sine, -1.0
+    ).reshape(tokens, q_width)
+    d_key_in = apply_rotary(
+        d_keys.reshape(tokens, KEY_VALUE_HEADS, HEAD_DIMENSION), cosine, sine, -1.0
+    ).reshape(tokens, kv_width)
+    d_qkv = jnp.concatenate([d_query_in, d_key_in, d_values.reshape(tokens, kv_width)], axis=1)
+    d_qkv = d_qkv.astype(jnp.bfloat16)
+    d_normed_one = narrow_exact(back_product(d_qkv, w_qkv), spread)
+    d_in_norm, d_attn_gain = norm_backward(d_normed_one, unit_one, scale_one, attn_gain)
+    input_grad = d_hidden + d_in_norm
+    attn_term = jnp.concatenate(
+        [weight_term(normed_one, d_qkv), weight_term(attended, d_branch)], axis=1
+    )
+    gains = jnp.concatenate([d_attn_gain, d_mlp_gain])
+    lanes = 128
+    gain_rows = -(-gains.shape[0] // (8 * lanes)) * 8
+    gains = jnp.pad(gains, (0, gain_rows * lanes - gains.shape[0])).reshape(gain_rows, lanes)
+
+    def split(term):
+        return term.reshape(PLANES, 2, 2, 2, term.shape[0] // devices, term.shape[1])
+
+    attn_part, gate_part, up_part, down_part, gain_sum = scatter_blocks(
+        [split(attn_term), split(gate_term), split(up_term), split(down_term)], gains, 1
+    )
+    attn_part = attn_part[:rows]
+    gain_sum = gain_sum.reshape(-1)
+    first, second = q_width, q_width + kv_width
+    third = second + kv_width
+    return (
+        output.reshape(inputs.shape),
+        input_grad.reshape(inputs.shape),
+        attn_part[:, :first].reshape(-1),
+        attn_part[:, first:second].reshape(-1),
+        attn_part[:, second:third].reshape(-1),
+        attn_part[:, third:].reshape(-1),
+        gate_part[:rows].reshape(-1),
+        up_part[:rows].reshape(-1),
+        down_part.reshape(-1),
+        gain_sum[:model_width],
+        gain_sum[model_width : 2 * model_width],
+    )
+
+
 def solution(mesh):
     in_specs = (
         P("fsdp", None, None),
@@ -308,4 +778,6 @@
         P(),
         P(),
     )
-    return jax.shard_map(body, mesh=mesh, in_specs=in_specs, out_specs=out_specs, check_vma=False)
+    chosen = fast_body if mesh.shape["fsdp"] == 8 * PLANES else body
+    return jax.shard_map(
+        chosen, mesh=mesh, in_specs=in_specs, out_specs=out_specs, check_vma=False)

time: 1060 us -> 485 us (0.46)
  waiting for transfers between devices: 620 us -> 0 us
  Pallas kernels: 0 us -> 386 us
  blocking collectives: 132 us -> 0 us
  other arithmetic: 124 us -> 9.2 us
  local copies, waits for them, and re-layouts: 105 us -> 32.9 us
  matrix products: 61.9 us -> 48.2 us
  between operations: 15 us -> 1.4 us
    unnamed x7 -> x0, waiting for transfers between devices: 518 us -> none
    pallas_call x0 -> x2, Pallas kernels: none -> 386 us  [the longest x1 203 us: scatter_blocks(): pl.pallas_call(functools.partial(scatter_kernel, count), out_shape=[jax.S...]
    all_gather x5 -> x0, waiting for transfers between devices: 102 us -> none  [the longest x1 52 us: body(): lax.all_gather(up_weight, 'fsdp', axis=0, tiled=True)]
    all_gather x2 -> x0, blocking collectives: 90 us -> none  [the longest x1 47.7 us: body(): lax.all_gather(value_matrix, 'fsdp', axis=0, tiled=True)]
    all_gather x4 -> x0, other arithmetic: 89.1 us -> none  [the longest x1 40.9 us: body(): lax.all_gather(query_weight, 'fsdp', axis=0, tiled=True)]
    another operation x7 -> x0, local copies, waits for them, and re-layouts: 47.9 us -> none  [flat_slice(): return product.reshape(count, stretch)]
    psum x1 -> x0, blocking collectives: 41.7 us -> none  [body(): gain_sums = lax.psum((d_attn_gain, d_mlp_gain), 'fsdp')]
    reshape x7 -> x14, local copies, waits for them, and re-layouts: 38.8 us -> 12.8 us  [the longest x6 5.74 us: lay(): return weight.reshape(rows, -1)]
  transfers between devices with their start and end apart: 6 -> 0, of which waited for: 3 -> 0; matrix products, arithmetic and copies ran while one was open for 14% -> 0% of each run, Pallas kernels for 0% -> 0%
where the time goes in v1:
time: 485 us; the launch traced here: 478 us
  Pallas kernels  386 us (80%)
  matrix products  48.2 us (10%)
  local copies, waits for them, and re-layouts  32.9 us (7%)
  other arithmetic  9.2 us (2%)
    pallas_call x1, Pallas kernels, scatter_blocks(): pl.pallas_call(functools.partial(scatter_kernel, count), out_shape=[jax.S...  203 us
    pallas_call x1, Pallas kernels, gather_blocks(): pl.pallas_call(functools.partial(gather_kernel, count), out_shape=[jax.Sh...  183 us
    dot_general x8, matrix products, matrix_product(): return jnp.dot(left, right, preferred_element_type=jnp.float32)  15.7 us
    dot_general x7, matrix products, back_product(): jnp.einsum('tf,df->td', left, right, preferred_element_type=jnp.float32)  15.6 us
    dot_general x5, matrix products, weight_term(): jnp.einsum('tr,tf->rf', left, right, preferred_element_type=jnp.float32)  13 us

profile of v1, /device:TPU:0, one launch (start us, length us, event | category | flops | bytes accessed | tf_op | source)
XLA Modules:
  0.0 477.6 jit_solution(16123677696097196555)
XLA Ops:
  0.6 1.1 fusion.64
  1.8 0.8 reshape.336
  2.6 0.8 reshape.337
  3.5 0.8 broadcast_multiply_fusion
  4.2 0.9 reshape.335
  5.2 0.9 reshape.338
  6.1 0.1 concatenate.47
  6.2 0.7 pad.14.refs_0_
  6.9 1.1 reshape.339
  8.0 0.7 pad.15.refs_1_
  8.7 1.1 reshape.340
  9.8 0.7 pad.16.refs_2_
  10.5 1.8 reshape.341.refs_3_
  12.2 2.0 fusion.29
  14.3 182.6 %shard_map.194 = (bf16[4,2,2,2,32,2560]{5,4,3,2,1,0:T(8,128)(2,1)}, bf16[4,2,2,2,32,2560]{5,4,3,2,1,0:T(8,128)(2,1)}, bf16[4,2,2,2,32,2560]{5,4,3,2,1,0:T(8,128)(2,1)}, bf16[4,2,2,2,80,960]{5,4,3,2,1,0:T(8,128)(2,1)}) custom-call(bf16[32,2560]{1,0:T(8,128)(2,1)} %pad.14.refs_0_, bf16[32,2560]{1,0:T(8,128)(2,1)} %pad.15.refs_1_, ...), custom_call_target="tpu_custom_call" | custom-call | tf_op jit(solution)/shard_map/pallas_call | solution.py:389
  196.9 3.6 fusion.8
  200.8 0.6 copy-done.7
  201.3 0.4 fusion.104
  201.7 0.2 exponential_reduce_fusion
  201.9 0.1 exponential_convert_fusion
  202.1 0.2 convolution_convert_fusion.5
  202.3 0.2 copy-done.20
  202.5 0.9 fusion.30
  203.5 3.7 multiply_reduce_fusion.2
  207.2 1.1 fusion.31
  208.3 0.9 fusion.106
  209.2 0.9 fusion.105
  210.2 0.2 copy-done.4
  210.3 2.3 multiply_convert_fusion
  212.6 2.7 fusion.36
  215.4 1.8 fusion.107
  217.1 1.8 reduce-precision_convert_fusion.3
  219.0 1.2 fusion.2
  220.2 1.0 multiply_reduce_fusion
  221.2 0.2 multiply_add_fusion
  221.4 4.1 fusion.33
  225.5 1.3 fusion.37
  226.8 1.3 fusion.38
  228.2 1.0 fusion.65
  229.1 0.3 convolution_bitcast_fusion.3
  229.5 0.2 fusion.81
  229.9 3.2 reduce-precision_convert_fusion.1
  233.2 1.2 fusion
  234.5 0.4 fusion.63
  235.0 1.0 fusion.62
  236.0 0.7 convolution_convert_fusion.4
  236.7 1.0 convolution_convert_fusion.3
  237.7 3.2 pad_maximum_fusion
  240.8 8.0 %copy.27 = bf16[1024,2560]{1,0:T(8,128)(2,1)} copy(bf16[1024,2560]{0,1:T(8,128)(2,1)} %pad_maximum_fusion) | data formatting | bytes 10485760 | tf_op jit(solution)/shard_map/concatenate | solution.py:721
  248.9 3.7 convolution_convert_fusion.2
  252.6 7.9 %copy.28 = bf16[2560,960]{1,0:T(8,128)(2,1)} copy(bf16[2560,960]{0,1:T(8,128)(2,1)} %convolution_convert_fusion.2) | data formatting | bytes 9830400 | tf_op jit(solution)/shard_map/convert_element_type | solution.py:689
  260.4 3.8 convolution_convert_fusion
  264.3 3.9 convolution_convert_fusion.1
  268.1 203.3 %shard_map.195 = (f32[32,2560]{1,0:T(8,128)S(1)}, f32[32,2560]{1,0:T(8,128)S(1)}, f32[32,2560]{1,0:T(8,128)S(1)}, f32[80,960]{1,0:T(8,128)S(1)}, f32[16,128]{1,0:T(8,128)S(1)}) custom-call(bf16[4,2,2,2,32,2560]{5,4,3,2,1,0:T(8,128)(2,1)} %bitcast.143, bf16[4,2,2,2,32,2560]{5,4,3,2,1,0:T(8,128)(2,1)} %bitcast.134, bf16[4,2,2,2,32,2560]{5,4,3,2,1,0:T(8,128)(2,1)} %bitcast.133, ...), custom_call_target="tpu_custom_call" | custom-call | tf_op jit(solution)/shard_map/pallas_call | solution.py:549
  471.5 0.7 reshape.370
  472.2 0.7 reshape.371
  473.0 0.7 fusion.103
  473.6 0.1 fusion.102
  473.7 0.1 fusion.101
  473.8 0.8 reshape.369
  474.6 0.7 reshape.368
  475.3 0.7 reshape.367
  476.0 0.7 reshape.366
  476.7 0.9 reshape.372
  (87 shorter events, 0.6 us)
Async XLA Ops:
  1.7 198.7 %copy-start.26 = (f32[128]{0:T(128)}, f32[128]{0:T(128)S(1)}, u32[]{:S(2)}) copy-start(f32[128]{0:T(128)S(1)} %add_rsqrt_fusion.1) | copy-start | bytes 1540
  1.8 217.2 %copy-start.24 = (s32[960]{0:T(1024)}, s32[960]{0:T(1024)S(1)}, u32[]{:S(2)}) copy-start(s32[960]{0:T(1024)S(1)} %fusion.90) | copy-start | bytes 11524
  14.3 186.4 %copy-start.13 = (bf16[128,1024]{1,0:T(8,128)(2,1)}, bf16[128,1024]{1,0:T(8,128)(2,1)S(1)}, u32[]{:S(2)}) copy-start(bf16[128,1024]{1,0:T(8,128)(2,1)S(1)} %fusion.29) | copy-start | bytes 786436
  196.9 11.4 %slice-start = ((s8[5242880]{0:T(1024)(128)(4,1)}), s8[4194304]{0:T(1024)(128)(4,1)S(1)}, s32[]{:S(2)}) async-start(s8[5242880]{0:T(1024)(128)(4,1)} %bitcast.135), calls=%async_computation | async-start | bytes 8388608
  200.5 2.0 copy-start.6
  200.6 2.9 copy-start.2
  200.7 0.7 copy-start.7
  200.7 1.0 copy-start.9
  200.7 1.0 copy-start.15
  200.8 1.0 copy-start.17
  201.7 5.4 %copy-start.21 = (f32[960]{0:T(1024)S(1)}, f32[960]{0:T(1024)}, u32[]{:S(2)}) copy-start(f32[960]{0:T(1024)} %param.14) | copy-start | bytes 11524
  201.7 6.6 %slice-start.1 = ((s8[5242880]{0:T(1024)(128)(4,1)}), s8[1048576]{0:T(1024)(128)(4,1)S(1)}, s32[]{:S(2)}) async-start(s8[5242880]{0:T(1024)(128)(4,1)} %bitcast.135), calls=%async_computation.1 | async-start | bytes 2097152
  201.9 0.6 copy-start.20
  202.1 7.1 %slice-start.2 = ((s8[5242880]{0:T(1024)(128)(4,1)}), s8[4194304]{0:T(1024)(128)(4,1)S(1)}, s32[]{:S(2)}) async-start(s8[5242880]{0:T(1024)(128)(4,1)} %bitcast.139), calls=%async_computation.2 | async-start | bytes 8388608
  203.5 3.7 copy-start.11
  207.2 2.1 slice-start.3
  207.2 2.9 slice-start.4
  208.3 1.8 slice-start.5
  209.2 1.1 copy-start.4
  212.6 4.5 copy-start
  225.5 3.7 copy-start.8
  225.5 3.7 copy-start.10
  225.5 4.0 copy-start.16
  225.5 4.0 copy-start.18
  225.5 4.3 copy-start.19
  229.8 3.4 copy-start.25
  233.2 1.3 copy-start.3
  233.2 1.3 copy-start.22
  233.2 1.3 copy-start.27
  233.2 1.7 copy-start.23
  233.2 2.8 copy-start.12
  234.5 2.1 copy-start.14
  240.8 8.0 %copy-start.1 = (bf16[128,2560]{1,0:T(8,128)(2,1)S(1)}, bf16[128,2560]{1,0:T(8,128)(2,1)}, u32[]{:S(2)}) copy-start(bf16[128,2560]{1,0:T(8,128)(2,1)} %copy-done) | copy-start | bytes 1966084
  240.8 8.0 %copy-start.5 = (bf16[1,128,960]{1,2,0:T(8,128)(2,1)S(1)}, bf16[1,128,960]{1,2,0:T(8,128)(2,1)}, u32[]{:S(2)}) copy-start(bf16[1,128,960]{1,2,0:T(8,128)(2,1)} %param.12) | copy-start | bytes 737284

commit v2 on v1

--- a/solution.py
+++ b/solution.py
@@ -332,56 +332,95 @@
     me = lax.axis_index("fsdp")
     z, y, x, c = unit_place(me)
     meet(partners(me))
-
-    def copies(a, phase):
-        whole = wholes[a]
-        x_first = a % 2 == 0
-        if phase == 0:
-            return [
-                remote(
-                    shards[a],
-                    whole.at[z, y, x, c],
-                    send.at[a, k - 1],
-                    receive.at[a, k - 1],
-                    unit_index((z + k) % PLANES, y, x, c),
-                )
-                for k in range(1, PLANES)
-            ]
-        over_x = unit_index(z, y, 1 - x, c)
-        over_y = unit_index(z, 1 - y, x, c)
-        if phase == 1:
-            part, device = whole.at[:, y, x, c], (over_x if x_first else over_y)
-        elif phase == 2:
-            part = whole.at[:, y, :, c] if x_first else whole.at[:, :, x, c]
-            device = over_y if x_first else over_x
+    over_x = unit_index(z, y, 1 - x, c)
+    over_y = unit_index(z, 1 - y, x, c)
+
+    def plane(k):
+        return (z + PLANES - k) % PLANES
+
+    def copy(a, slot, source, target, device):
+        return remote(source, target, send.at[a, slot], receive.at[a, slot], device)
+
+    def along_z(a, k):
+        device = unit_index((z + k) % PLANES, y, x, c)
+        return copy(a, k - 1, shards[a], wholes[a].at[z, y, x, c], device)
+
+    def own(a, k, slot, device):
+        target = wholes[a].at[plane(k), y, x, c]
+        return copy(a, slot + k, shards[a] if k == 0 else target, target, device)
+
+    def first(a, k):
+        return own(a, k, 3, over_x if a % 2 == 0 else over_y)
+
+    def second(a, k):
+        return own(a, k, 7, over_y if a % 2 == 0 else over_x)
+
+    def forward(a, k):
+        if a % 2 == 0:
+            part, device = wholes[a].at[plane(k), y, 1 - x, c], over_y
         else:
-            part, device = whole.at[:, :, :, c], unit_index(z, y, x, 1 - c)
-        return [remote(part, part, send.at[a, phase + 2], receive.at[a, phase + 2], device)]
+            part, device = wholes[a].at[plane(k), 1 - y, x, c], over_x
+        return copy(a, 11 + k, part, part, device)
+
+    def across(a):
+        part = wholes[a].at[:, :, :, c]
+        return copy(a, 15, part, part, unit_index(z, y, x, 1 - c))
 
     locals_ = [
         pltpu.make_async_copy(shards[a], wholes[a].at[z, y, x, c], local.at[a])
         for a in range(count)
     ]
+
+    def begin(a):
+        first(a, 0).start()
+        second(a, 0).start()
+        locals_[a].start()
+
+    def pass_on(a):
+        for k in range(1, PLANES):
+            first(a, k).wait_recv()
+            forward(a, k).start()
+
+    def finish(a):
+        for k in range(PLANES):
+            second(a, k).wait_recv()
+            forward(a, k).wait_recv()
+        locals_[a].wait()
+        across(a).start()
+
+    for k in range(1, PLANES):
+        along_z(0, k).start()
+    begin(0)
+    begin(1)
     for a in range(count):
-        for copy in copies(a, 0):
-            copy.start()
-        locals_[a].start()
-    for step in range(count + 3):
-        for phase in (3, 2, 1):
-            a = step - (phase - 1)
-            if 0 <= a < count:
-                if phase == 1:
-                    locals_[a].wait()
-                for copy in copies(a, phase - 1):
-                    copy.wait_recv()
-                for copy in copies(a, phase):
-                    copy.start()
+        for k in range(1, PLANES):
+            along_z(a, k).wait_recv()
+        if a + 1 < count:
+            for k in range(1, PLANES):
+                along_z(a + 1, k).start()
+        for k in range(1, PLANES):
+            first(a, k).start()
+            second(a, k).start()
+        if a + 2 < count:
+            begin(a + 2)
+        first(a, 0).wait_recv()
+        forward(a, 0).start()
+        if a >= 1:
+            pass_on(a - 1)
+        if a >= 2:
+            finish(a - 2)
+    pass_on(count - 1)
+    finish(count - 2)
+    finish(count - 1)
     for a in range(count):
-        for copy in copies(a, 3):
-            copy.wait_recv()
-        for phase in range(4):
-            for copy in copies(a, phase):
-                copy.wait_send()
+        across(a).wait_recv()
+        across(a).wait_send()
+        for k in range(PLANES):
+            if k > 0:
+                along_z(a, k).wait_send()
+            first(a, k).wait_send()
+            second(a, k).wait_send()
+            forward(a, k).wait_send()
 
 
 def gather_blocks(shards, identity):
@@ -392,86 +431,110 @@
         in_specs=[pl.BlockSpec(memory_space=pl.ANY)] * count,
         out_specs=[pl.BlockSpec(memory_space=pl.ANY)] * count,
         scratch_shapes=[
-            pltpu.SemaphoreType.DMA((count, 6)),
-            pltpu.SemaphoreType.DMA((count, 6)),
+            pltpu.SemaphoreType.DMA((count, 16)),
+            pltpu.SemaphoreType.DMA((count, 16)),
             pltpu.SemaphoreType.DMA((count,)),
         ],
         compiler_params=pltpu.CompilerParams(collective_id=identity, has_side_effects=True),
     )(*shards)
 
 
-def scatter_kernel(count, *refs):
-    grads, gain = refs[:count], refs[count]
-    outs, gain_out = refs[count + 1 : 2 * count + 1], refs[2 * count + 1]
-    rest = refs[2 * count + 2 :]
-    held, sibling, second, third, last = (rest[i * count : (i + 1) * count] for i in range(5))
-    gain_a, gain_b, gain_c, gain_z, send, receive, local = rest[5 * count :]
+def column_tiles(width, tile):
+    return [(start, min(tile, width - start)) for start in range(0, width, tile)]
+
+
+def scatter_kernel(plan, *refs):
+    count = len(plan)
+    factors = []
+    used = 0
+    for terms in plan:
+        factors.append([(refs[used + 2 * i], refs[used + 2 * i + 1], at) for i, at in enumerate(terms)])
+        used += 2 * len(terms)
+    gain = refs[used]
+    outs, gain_out = refs[used + 1 : used + 1 + count], refs[used + 1 + count]
+    rest = refs[used + 2 + count :]
+    grads, sibling, second, third, last = (rest[i * count : (i + 1) * count] for i in range(5))
+    gain_a, gain_b, gain_c, gain_z, send, receive = rest[5 * count :]
     me = lax.axis_index("fsdp")
     z, y, x, c = unit_place(me)
-    meet(partners(me))
     over_core = unit_index(z, y, x, 1 - c)
     over_x = unit_index(z, y, 1 - x, c)
     over_y = unit_index(z, 1 - y, x, c)
-
-    def copies(a, phase):
-        x_first = a % 2 == 0
-        if phase == 0:
-            jobs = [(grads[a].at[:, :, :, 1 - c], sibling[a], over_core)]
-        elif phase == 1:
-            if x_first:
-                jobs = [(held[a].at[:, :, 1 - x], second[a], over_x)]
-            else:
-                jobs = [(held[a].at[:, 1 - y], second[a], over_y)]
-        elif phase == 2:
-            if x_first:
-                jobs = [(held[a].at[:, 1 - y, x], third[a], over_y)]
-            else:
-                jobs = [(held[a].at[:, y, 1 - x], third[a], over_x)]
-        else:
-            jobs = []
-            for k in range(1, PLANES):
-                to = (z + k) % PLANES
-                jobs.append((held[a].at[to, y, x], last[a].at[k - 1], unit_index(to, y, x, c)))
-        return [
-            remote(s, d, send.at[a, phase + i], receive.at[a, phase + i], device)
-            for i, (s, d, device) in enumerate(jobs)
-        ]
+    meet(partners(me))
+
+    def build(a):
+        rows = grads[a].shape[4]
+
+        @pl.loop(0, PLANES)
+        def _(zz):
+            for left, right, at in factors[a]:
+                part = left[pl.ds(pl.multiple_of(zz * (8 * rows), 8 * rows), 8 * rows), :]
+                for start, width in column_tiles(right.shape[1], 512):
+                    value = jnp.dot(
+                        part, right[:, start : start + width], preferred_element_type=jnp.float32
+                    )
+                    grads[a][zz, :, :, :, :, at + start : at + start + width] = value.astype(
+                        grads[a].dtype
+                    ).reshape(2, 2, 2, rows, width)
+
+    def plane(k):
+        return (z + k) % PLANES
+
+    def copy(a, slot, source, target, device):
+        return remote(source, target, send.at[a, slot], receive.at[a, slot], device)
+
+    def across(a):
+        return copy(a, 0, grads[a].at[:, :, :, 1 - c], sibling[a], over_core)
+
+    def first(a, k):
+        zz = plane(k)
+        if a % 2 == 0:
+            return copy(a, 1 + k, grads[a].at[zz, :, 1 - x, c], second[a].at[zz], over_x)
+        return copy(a, 1 + k, grads[a].at[zz, 1 - y, :, c], second[a].at[zz], over_y)
+
+    def after(a, k):
+        zz = plane(k)
+        if a % 2 == 0:
+            return copy(a, 5 + k, grads[a].at[zz, 1 - y, x, c], third[a].at[zz], over_y)
+        return copy(a, 5 + k, grads[a].at[zz, y, 1 - x, c], third[a].at[zz], over_x)
+
+    def along_z(a, k):
+        zz = plane(k)
+        device = unit_index(zz, y, x, c)
+        return copy(a, 8 + k, grads[a].at[zz, y, x, c], last[a].at[k - 1], device)
 
     def add(target, term):
         target[...] = (target[...].astype(jnp.float32) + term[...].astype(jnp.float32)).astype(
             target.dtype
         )
 
-    def fold(a, phase):
-        x_first = a % 2 == 0
-        if phase == 0:
-
-            @pl.loop(0, PLANES * 4)
-            def _(i):
-                zz, yy, xx = i // 4, (i // 2) % 2, i % 2
-                add(held[a].at[zz, yy, xx], sibling[a].at[zz, yy, xx])
-
-        elif phase == 1:
-
-            @pl.loop(0, PLANES * 2)
-            def _(i):
-                zz, other = i // 2, i % 2
-                if x_first:
-                    add(held[a].at[zz, other, x], second[a].at[zz, other])
-                else:
-                    add(held[a].at[zz, y, other], second[a].at[zz, other])
-
-        elif phase == 2:
-
-            @pl.loop(0, PLANES)
-            def _(zz):
-                add(held[a].at[zz, y, x], third[a].at[zz])
-
-        else:
-            total = held[a][z, y, x].astype(jnp.float32)
-            for k in range(PLANES - 1):
-                total = total + last[a][k].astype(jnp.float32)
-            outs[a][...] = total
+    def fold_core(a):
+        across(a).wait_recv()
+
+        @pl.loop(0, PLANES * 4)
+        def _(i):
+            zz, yy, xx = i // 4, (i // 2) % 2, i % 2
+            add(grads[a].at[zz, yy, xx, c], sibling[a].at[zz, yy, xx])
+
+    def fold_first(a, k):
+        first(a, k).wait_recv()
+        zz = plane(k)
+
+        @pl.loop(0, 2)
+        def _(other):
+            if a % 2 == 0:
+                add(grads[a].at[zz, other, x, c], second[a].at[zz, other])
+            else:
+                add(grads[a].at[zz, y, other, c], second[a].at[zz, other])
+
+        after(a, k).start()
+
+    def fold_after(a, k):
+        after(a, k).wait_recv()
+        zz = plane(k)
+        add(grads[a].at[zz, y, x, c], third[a].at[zz])
+        if k > 0:
+            along_z(a, k).start()
 
     def gain_copies(phase):
         if phase < 3:
@@ -480,18 +543,15 @@
                 (gain_a.at[0], gain_b.at[1], over_x),
                 (gain_b.at[0], gain_c, over_y),
             )[phase]
-            jobs = [(source, target, device)]
-        else:
-            jobs = [
-                (gain_z.at[z], gain_z.at[z], unit_index((z + k) % PLANES, y, x, c))
-                for k in range(1, PLANES)
-            ]
+            return [copy(count, phase, source, target, device)]
         return [
-            remote(s, d, send.at[count, phase + i], receive.at[count, phase + i], device)
-            for i, (s, d, device) in enumerate(jobs)
+            copy(count, 2 + k, gain_z.at[z], gain_z.at[z], unit_index(plane(k), y, x, c))
+            for k in range(1, PLANES)
         ]
 
-    def gain_fold(phase):
+    def gain_step(phase):
+        for part in gain_copies(phase):
+            part.wait_recv()
         if phase == 0:
             gain_a[0] = gain[...] + gain_a[1]
         elif phase == 1:
@@ -500,59 +560,82 @@
             gain_z[z] = gain_b[0] + gain_c[...]
         else:
             gain_out[...] = (gain_z[0] + gain_z[1]) + (gain_z[2] + gain_z[3])
-
-    locals_ = [
-        pltpu.make_async_copy(grads[a].at[:, :, :, c], held[a], local.at[a]) for a in range(count)
+        if phase < 3:
+            for part in gain_copies(phase + 1):
+                part.start()
+
+    gain_copies(0)[0].start()
+    items = [
+        (a, k) for pair in range(0, count, 2) for k in (1, 2, 3, 0) for a in (pair, pair + 1)
     ]
-    for copy in gain_copies(0):
-        copy.start()
+    window = 4
+    folded = set()
+
+    def release(item):
+        if item[0] not in folded:
+            fold_core(item[0])
+            folded.add(item[0])
+        first(*item).start()
+
+    for a in range(2):
+        build(a)
+        across(a).start()
+    for item in items[:window]:
+        release(item)
+    for a in range(2, count):
+        build(a)
+        across(a).start()
+    for i, item in enumerate(items):
+        fold_first(*item)
+        if i + window < len(items):
+            release(items[i + window])
+        if i >= 2:
+            fold_after(*items[i - 2])
+        if i % 3 == 2 and i // 3 < 4:
+            gain_step(i // 3)
+    for item in items[-2:]:
+        fold_after(*item)
     for a in range(count):
-        for copy in copies(a, 0):
-            copy.start()
-        locals_[a].start()
-    for step in range(count + 3):
-        for phase in (3, 2, 1, 0):
-            a = step - phase
-            if 0 <= a < count:
-                if phase == 0:
-                    locals_[a].wait()
-                for copy in copies(a, phase):
-                    copy.wait_recv()
-                fold(a, phase)
-                if phase < 3:
-                    for copy in copies(a, phase + 1):
-                        copy.start()
-        if step < 4:
-            for copy in gain_copies(step):
-                copy.wait_recv()
-            gain_fold(step)
-            if step < 3:
-                for copy in gain_copies(step + 1):
-                    copy.start()
+        total = grads[a][z, y, x, c].astype(jnp.float32)
+        for k in range(1, PLANES):
+            along_z(a, k).wait_recv()
+            total = total + last[a][k - 1].astype(jnp.float32)
+        outs[a][...] = total
+    for a in range(count):
+        across(a).wait_send()
+        for k in range(PLANES):
+            first(a, k).wait_send()
+            after(a, k).wait_send()
+            if k > 0:
+                along_z(a, k).wait_send()
     for phase in range(4):
-        for a in range(count):
-            for copy in copies(a, phase):
-                copy.wait_send()
-        for copy in gain_copies(phase):
-            copy.wait_send()
-
-
-def scatter_blocks(grads, gain, identity):
-    count = len(grads)
-    blocks = [g.shape[4:] for g in grads]
-    kind = grads[0].dtype
+        for part in gain_copies(phase):
+            part.wait_send()
+
+
+def scatter_products(products, gain, devices, identity):
+    plan, operands, blocks = [], [], []
+    for terms in products:
+        offsets, at = [], 0
+        for left, right in terms:
+            offsets.append(at)
+            at += right.shape[1]
+            operands += [left.T, right]
+        plan.append(tuple(offsets))
+        blocks.append((terms[0][0].shape[1] // devices, at))
+    count = len(plan)
     vmem = pl.BlockSpec(memory_space=pltpu.VMEM)
 
     def room(lead):
-        return [pltpu.VMEM(lead + b, kind) for b in blocks]
+        return [pltpu.VMEM(lead + b, jnp.bfloat16) for b in blocks]
 
     return pl.pallas_call(
-        functools.partial(scatter_kernel, count),
+        functools.partial(scatter_kernel, tuple(plan)),
         out_shape=[jax.ShapeDtypeStruct(b, jnp.float32) for b in blocks]
         + [jax.ShapeDtypeStruct(gain.shape, gain.dtype)],
-        in_specs=[pl.BlockSpec(memory_space=pl.ANY)] * count + [vmem],
+        in_specs=[vmem] * (len(operands) + 1),
         out_specs=[vmem] * (count + 1),
-        scratch_shapes=room((PLANES, 2, 2))
+        scratch_shapes=room((PLANES, 2, 2, 2))
         + room((PLANES, 2, 2))
         + room((PLANES, 2))
         + room((PLANES,))
@@ -562,14 +645,13 @@
             pltpu.VMEM((2,) + gain.shape, gain.dtype),
             pltpu.VMEM(gain.shape, gain.dtype),
             pltpu.VMEM((PLANES,) + gain.shape, gain.dtype),
-            pltpu.SemaphoreType.DMA((count + 1, 6)),
-            pltpu.SemaphoreType.DMA((count + 1, 6)),
-            pltpu.SemaphoreType.DMA((count,)),
+            pltpu.SemaphoreType.DMA((count + 1, 12)),
+            pltpu.SemaphoreType.DMA((count + 1, 12)),
         ],
         compiler_params=pltpu.CompilerParams(
-            collective_id=identity, has_side_effects=True, vmem_limit_bytes=48 * 1024 * 1024
+            collective_id=identity, has_side_effects=True, vmem_limit_bytes=56 * 1024 * 1024
         ),
-    )(*grads, gain)
+    )(*operands, gain)
 
 
 def spread_matrix(width, rows, padded_rows, devices):
@@ -625,9 +707,17 @@
     def fill(matrix):
         return jnp.pad(matrix, ((0, padded - rows), (0, 0)))
 
+    qkv_width = q_width + 2 * kv_width
+    gap = -qkv_width % 128
     attn_shard = fill(
         jnp.concatenate(
-            [lay(query_weight), lay(key_matrix), lay(value_matrix), lay(output_weight)], axis=1
+            [
+                lay(query_weight),
+                lay(key_matrix),
+                jnp.pad(lay(value_matrix), ((0, 0), (0, gap))),
+                lay(output_weight),
+            ],
+            axis=1,
         )
     )
     gathered = gather_blocks(
@@ -640,8 +730,8 @@
         0,
     )
     attn_all, w_gate, w_up, w_down = (g.reshape(-1, g.shape[-1]) for g in gathered)
-    w_qkv = attn_all[:, : q_width + 2 * kv_width]
-    w_output = attn_all[:, q_width + 2 * kv_width :]
+    w_qkv = attn_all[:, :qkv_width]
+    w_output = attn_all[:, qkv_width + gap :]
 
     x = inputs.reshape(tokens, model_width).astype(jnp.float32)
     cotangent = out_cotangent.reshape(tokens, model_width)
@@ -685,14 +775,6 @@
     )
     d_up = (d_mixed * activated).astype(jnp.bfloat16)
 
-    def weight_term(left, right):
-        return jnp.einsum("tr,tf->rf", left, right, preferred_element_type=jnp.float32).astype(
-            jnp.bfloat16
-        )
-
-    gate_term = weight_term(normed_two, d_gate)
-    up_term = weight_term(normed_two, d_up)
-    down_term = weight_term(mixed, cotangent)
     d_normed_two = narrow_exact(back_product(d_gate, w_gate) + back_product(d_up, w_up), spread)
     d_hid_norm, d_mlp_gain = norm_backward(d_normed_two, unit_two, scale_two, mlp_gain)
     d_hidden = cotangent.astype(jnp.float32) + d_hid_norm
@@ -718,19 +800,19 @@
     d_normed_one = narrow_exact(back_product(d_qkv, w_qkv), spread)
     d_in_norm, d_attn_gain = norm_backward(d_normed_one, unit_one, scale_one, attn_gain)
     input_grad = d_hidden + d_in_norm
-    attn_term = jnp.concatenate(
-        [weight_term(normed_one, d_qkv), weight_term(attended, d_branch)], axis=1
-    )
     gains = jnp.concatenate([d_attn_gain, d_mlp_gain])
     lanes = 128
     gain_rows = -(-gains.shape[0] // (8 * lanes)) * 8
     gains = jnp.pad(gains, (0, gain_rows * lanes - gains.shape[0])).reshape(gain_rows, lanes)
 
-    def split(term):
-        return term.reshape(PLANES, 2, 2, 2, term.shape[0] // devices, term.shape[1])
-
-    attn_part, gate_part, up_part, down_part, gain_sum = scatter_blocks(
-        [split(attn_term), split(gate_term), split(up_term), split(down_term)], gains, 1
+    products = [
+        [(normed_two, d_gate)],
+        [(normed_two, d_up)],
+        [(mixed, cotangent)],
+        [(normed_one, jnp.pad(d_qkv, ((0, 0), (0, gap)))), (attended, d_branch)],
+    ]
+    gate_part, up_part, down_part, attn_part, gain_sum = scatter_products(
+        products, gains, devices, 1
     )
     attn_part = attn_part[:rows]
     gain_sum = gain_sum.reshape(-1)
@@ -742,7 +824,7 @@
         attn_part[:, :first].reshape(-1),
         attn_part[:, first:second].reshape(-1),
         attn_part[:, second:third].reshape(-1),
-        attn_part[:, third:].reshape(-1),
+        attn_part[:, third + gap :].reshape(-1),
         gate_part[:rows].reshape(-1),
         up_part[:rows].reshape(-1),
         down_part.reshape(-1),

time: 485 us -> 299 us (0.62); the launches traced: 478 us -> 298 us
  Pallas kernels: 386 us -> 225 us
  local copies, waits for them, and re-layouts: 32.9 us -> 23.1 us
  matrix products: 48.2 us -> 40.7 us
    pallas_call x1, Pallas kernels: 203 us -> 117 us  [scatter_products(): pl.pallas_call(functools.partial(scatter_kernel, tuple(plan)), out_shape=...]
    pallas_call x1, Pallas kernels: 183 us -> 108 us  [gather_blocks(): pl.pallas_call(functools.partial(gather_kernel, count), out_shape=[jax.Sh...]
    dot_general x5 -> x0, matrix products: 13 us -> none  [weight_term(): jnp.einsum('tr,tf->rf', left, right, preferred_element_type=jnp.float32)]
    concatenate x2, local copies, waits for them, and re-layouts: 8.15 us -> 0.25 us  [the longest x1 0.15 us: fast_body(): jnp.concatenate([d_query_in, d_key_in, d_values.reshape(tokens, kv_width)...]
    convert_element_type x1 -> x0, local copies, waits for them, and re-layouts: 7.88 us -> none  [weight_term(): jnp.einsum('tr,tf->rf', left, right, preferred_element_type=jnp.float32)]
    dot_general x7, matrix products: 15.6 us -> 21.2 us  [back_product(): jnp.einsum('tf,df->td', left, right, preferred_element_type=jnp.float32)]
    unnamed x68 -> x124, local copies, waits for them, and re-layouts: 1.14 us -> 6.42 us
    reshape x6, local copies, waits for them, and re-layouts: 5.74 us -> 0.82 us  [lay(): return weight.reshape(rows, -1)]
where the time goes in v2:
time: 299 us; the launch traced here: 298 us
  Pallas kernels  225 us (75%)
  matrix products  40.7 us (14%)
  local copies, waits for them, and re-layouts  23.1 us (8%)
  other arithmetic  7.3 us (2%)
    pallas_call x1, Pallas kernels, scatter_products(): pl.pallas_call(functools.partial(scatter_kernel, tuple(plan)), out_shape=...  117 us
    pallas_call x1, Pallas kernels, gather_blocks(): pl.pallas_call(functools.partial(gather_kernel, count), out_shape=[jax.Sh...  108 us
    dot_general x7, matrix products, back_product(): jnp.einsum('tf,df->td', left, right, preferred_element_type=jnp.float32)  21.2 us
    dot_general x8, matrix products, matrix_product(): return jnp.dot(left, right, preferred_element_type=jnp.float32)  16.8 us
    unnamed x124, local copies, waits for them, and re-layouts  6.42 us

profile of v2, /device:TPU:0, one launch (start us, length us, event | category | flops | bytes accessed | tf_op | source)
XLA Modules:
  0.0 297.8 jit_solution(17052456755450460552)
XLA Ops:
  0.7 1.1 copy.55
  2.0 2.2 fusion.34
  4.8 0.7 pad.24.refs_0_
  5.5 0.2 reshape.327
  5.7 0.7 pad.25.refs_1_
  6.4 0.2 reshape.328
  6.6 0.7 pad.26.refs_2_
  7.3 0.8 reshape.329.refs_3_
  8.1 107.6 %shard_map.194 = (bf16[4,2,2,2,32,2624]{5,4,3,2,1,0:T(8,128)(2,1)}, bf16[4,2,2,2,32,2560]{5,4,3,2,1,0:T(8,128)(2,1)}, bf16[4,2,2,2,32,2560]{5,4,3,2,1,0:T(8,128)(2,1)}, bf16[4,2,2,2,80,960]{5,4,3,2,1,0:T(8,128)(2,1)}) custom-call(bf16[32,2624]{1,0:T(8,128)(2,1)} %pad.24.refs_0_, bf16[32,2560]{1,0:T(8,128)(2,1)} %pad.25.refs_1_, ...), custom_call_target="tpu_custom_call" | custom-call | tf_op jit(solution)/shard_map/pallas_call | solution.py:428
  115.7 3.5 %fusion.8 = f32[128,1600]{0,1:T(8,128)S(1)} fusion(bf16[128,1024]{0,1:T(8,128)(2,1)S(1)} %fusion.34, bf16[1024,2624]{1,0:T(8,128)(2,1)} %bitcast.162), kind=kOutput, calls=%fused_computation.10 | convolution fusion | flops 419430400 | bytes 4489216 | tf_op jit(solution)/shard_map/dot_general | solution.py:54
  119.3 0.8 broadcast_multiply_fusion
  120.3 0.4 fusion.105
  120.7 0.2 exponential_reduce_fusion
  120.9 0.6 copy-done.31
  121.5 0.1 exponential_convert_fusion
  121.6 0.2 convolution_convert_fusion
  121.9 1.4 fusion.35
  123.3 2.2 multiply_reduce_fusion.2
  125.6 1.4 fusion.36
  127.2 0.9 fusion.107
  128.1 2.0 fusion.106
  130.1 3.2 %fusion.38 = bf16[1,128,960]{2,1,0:T(8,128)(2,1)} fusion(f32[128,960]{1,0:T(8,128)S(1)} %get-tuple-element.85, bf16[2560,960]{1,0:T(8,128)(2,1)S(1)} %bitcast.183, f32[128,2560]{1,0:T(8,128)S(1)} %fusion.107, f32[128,2560]{1,0:T(8,128)} %fusion.106), kind=kOutput, calls=%fused_computation.50 | convolution fusion | flops 631357440 | bytes 8273920 | tf_op jit(solution)/shard_map/dot_general | solution.py:54
  133.3 1.8 copy.78
  135.1 5.7 %multiply_convert_fusion = (bf16[128,2560]{1,0:T(8,128)(2,1)S(1)}, bf16[128,2560]{1,0:T(8,128)(2,1)S(1)}) fusion(f32[128,2560]{1,0:T(8,128)} %fusion.106, f32[128,2560]{1,0:T(8,128)} %copy-done, bf16[2560,960]{1,0:T(8,128)(2,1)} %bitcast.180, bf16[1,128,960]{1,2,0:T(8,128)(2,1)S(1)} %copy-done.22), kind=kOutput, calls=%fused_computation.32 | convolution fusion | flops 633405440 | bytes 9093120 | tf_op jit(solution)/shard_map/tf,df->td/dot_general | solution.py:58
  140.8 4.7 %fusion.108 = f32[128,1024]{1,0:T(8,128)S(1)} fusion(bf16[128,2560]{1,0:T(8,128)(2,1)S(1)} %get-tuple-element.58.refs_1_, bf16[1024,2560]{1,0:T(8,128)(2,1)} %bitcast.149), kind=kOutput, calls=%fused_computation.165 | convolution fusion | flops 671088640 | bytes 6422528 | tf_op jit(solution)/shard_map/tf,df->td/dot_general | solution.py:58
  145.6 1.8 reduce-precision_convert_fusion.3
  147.5 1.2 fusion.2
  148.7 0.8 multiply_reduce_fusion
  149.5 0.6 broadcast_multiply_fusion.2
  150.1 0.1 copy.62
  150.2 0.9 fusion.99.refs_9_
  151.2 3.2 %fusion.37 = bf16[128,960]{0,1:T(8,128)(2,1)S(1)} fusion(s32[960]{0:T(1024)} %copy-done.46, bf16[128,960]{1,0:T(8,128)(2,1)S(1)} %fusion.99.refs_9_, bf16[1024,2624]{1,0:T(8,128)(2,1)} %bitcast.164), kind=kOutput, calls=%fused_computation.48 | convolution fusion | flops 504553472 | bytes 2592768 | tf_op jit(solution)/shard_map/tf,df->td/dot_general | solution.py:58
  154.5 1.2 fusion.42
  155.8 0.2 fusion.71
  156.0 0.5 copy-done.24
  156.5 0.2 fusion.82
  156.9 0.1 copy.70
  157.0 0.4 copy-done.12
  157.5 0.3 convolution_bitcast_fusion.3
  157.8 0.7 subtract_convert_fusion.2
  158.7 0.3 fusion.41
  159.2 0.1 concatenate.52
  159.4 3.4 %reduce-precision_convert_fusion.1 = (bf16[128,1024]{1,0:T(8,128)(2,1)S(1)}, bf16[128,1024]{1,0:T(8,128)(2,1)S(1)}, bf16[128,1024]{1,0:T(8,128)(2,1)S(1)}) fusion(bf16[128,1600]{1,0:T(8,128)(2,1)S(1)} %concatenate.52, bf16[1024,2624]{1,0:T(8,128)(2,1)} %bitcast.165), kind=kOutput, calls=%fused_computation.78 | convolution fusion | flops 420347904 | bytes 4603904 | tf_op jit(solution)/shard_map/tf,df->td/dot_general | solution.py:58
  162.8 1.2 fusion
  164.0 0.3 fusion.67
  164.4 0.6 copy-done.2
  165.0 0.3 fusion.66
  165.3 1.0 copy.79
  166.2 1.7 copy.77
  168.0 1.7 copy.76
  169.7 1.2 fusion.21.refs_4_
  170.9 0.8 pad.27.refs_7_
  171.7 0.7 fusion.83.refs_10_
  172.4 117.4 %shard_map.195 = (f32[32,2560]{1,0:T(8,128)}, f32[32,2560]{1,0:T(8,128)}, f32[80,960]{1,0:T(8,128)}, f32[32,2624]{1,0:T(8,128)}, f32[16,128]{1,0:T(8,128)}) custom-call(bf16[1024,128]{1,0:T(8,128)(2,1)} %bitcast.154, bf16[128,2560]{1,0:T(8,128)(2,1)} %copy-done.5, bf16[1024,128]{1,0:T(8,128)(2,1)} %bitcast.155, bf16[128,2560]{1,0:T(8,128)(2,1)} %copy-done.4, ...), custom_call_target="tpu_custom_call" | custom-call | tf_op jit(solution)/shard_map/pallas_call | solution.py:632
  289.8 1.1 fusion.102
  290.8 0.7 reshape.350
  291.6 1.0 fusion.103
  292.6 0.7 reshape.351
  293.3 0.7 reshape.352
  294.0 0.7 reshape.353
  294.8 0.7 reshape.354
  295.5 0.7 reshape.355
  296.2 0.9 reshape.356
  297.1 0.7 fusion.104
  (145 shorter events, 1.7 us)
Async XLA Ops:
  0.6 3.6 %copy-start.33 = (bf16[28800]{0:T(1024)(128)(2,1)S(1)}, bf16[28800]{0:T(1024)(128)(2,1)}, u32[]{:S(2)}) copy-start(bf16[28800]{0:T(1024)(128)(2,1)} %param.15) | copy-start | bytes 172804
  0.7 124.9 %copy-start.46 = (s32[960]{0:T(1024)}, s32[960]{0:T(1024)S(1)}, u32[]{:S(2)}) copy-start(s32[960]{0:T(1024)S(1)} %fusion.91) | copy-start | bytes 11524
  0.7 3.7 %copy-start.38 = (bf16[9600]{0:T(1024)(128)(2,1)S(1)}, bf16[9600]{0:T(1024)(128)(2,1)}, u32[]{:S(2)}) copy-start(bf16[9600]{0:T(1024)(128)(2,1)} %param.16) | copy-start | bytes 57604
  0.7 3.8 %copy-start.39 = (bf16[9600]{0:T(1024)(128)(2,1)S(1)}, bf16[9600]{0:T(1024)(128)(2,1)}, u32[]{:S(2)}) copy-start(bf16[9600]{0:T(1024)(128)(2,1)} %param.17) | copy-start | bytes 57604
  0.7 3.9 %copy-start.34 = (bf16[28800]{0:T(1024)(128)(2,1)S(1)}, bf16[28800]{0:T(1024)(128)(2,1)}, u32[]{:S(2)}) copy-start(bf16[28800]{0:T(1024)(128)(2,1)} %param.18) | copy-start | bytes 172804
  2.0 2.6 copy-start.49
  2.0 3.5 %copy-start.27 = (bf16[76800]{0:T(1024)(128)(2,1)S(1)}, bf16[76800]{0:T(1024)(128)(2,1)}, u32[]{:S(2)}) copy-start(bf16[76800]{0:T(1024)(128)(2,1)} %param.19) | copy-start | bytes 460804
  2.0 4.4 %copy-start.28 = (bf16[76800]{0:T(1024)(128)(2,1)S(1)}, bf16[76800]{0:T(1024)(128)(2,1)}, u32[]{:S(2)}) copy-start(bf16[76800]{0:T(1024)(128)(2,1)} %param.20) | copy-start | bytes 460804
  4.2 111.5 %copy-start.21 = (bf16[128,1024]{0,1:T(8,128)(2,1)}, bf16[128,1024]{0,1:T(8,128)(2,1)S(1)}, u32[]{:S(2)}) copy-start(bf16[128,1024]{0,1:T(8,128)(2,1)S(1)} %fusion.34) | copy-start | bytes 786436
  4.2 3.1 %copy-start.29 = (bf16[76800]{0:T(1024)(128)(2,1)S(1)}, bf16[76800]{0:T(1024)(128)(2,1)}, u32[]{:S(2)}) copy-start(bf16[76800]{0:T(1024)(128)(2,1)} %param.21) | copy-start | bytes 460804
  115.7 11.4 %slice-start = ((s8[5242880]{0:T(1024)(128)(4,1)}), s8[1048576]{0:T(1024)(128)(4,1)S(1)}, s32[]{:S(2)}) async-start(s8[5242880]{0:T(1024)(128)(4,1)} %bitcast.143), calls=%async_computation | async-start | bytes 2097152
  119.2 2.4 copy-start.10
  120.1 0.7 copy-start.15
  120.2 0.7 copy-start.11
  120.2 0.7 copy-start.13
  120.2 0.6 copy-start.23
  120.2 0.6 copy-start.25
  120.6 6.5 %slice-start.1 = ((s8[5242880]{0:T(1024)(128)(4,1)}), s8[4194304]{0:T(1024)(128)(4,1)S(1)}, s32[]{:S(2)}) async-start(s8[5242880]{0:T(1024)(128)(4,1)} %bitcast.143), calls=%async_computation.1 | async-start | bytes 8388608
  120.9 0.6 copy-start.31
  121.9 6.2 %slice-start.4 = ((s8[5242880]{0:T(1024)(128)(4,1)}), s8[4194304]{0:T(1024)(128)(4,1)S(1)}, s32[]{:S(2)}) async-start(s8[5242880]{0:T(1024)(128)(4,1)} %bitcast.150), calls=%async_computation.4 | async-start | bytes 8388608
  123.3 2.3 copy-start.9
  123.3 2.3 copy-start.35
  125.6 1.5 copy-start.43
  125.6 2.5 slice-start.5
  125.6 4.4 %slice-start.6 = ((s8[5242880]{0:T(1024)(128)(4,1)}), s8[4194304]{0:T(1024)(128)(4,1)S(1)}, s32[]{:S(2)}) async-start(s8[5242880]{0:T(1024)(128)(4,1)} %bitcast.181), calls=%async_computation.6 | async-start | bytes 8388608
  127.1 1.0 copy-start.3
  127.1 2.9 slice-start.7
  128.0 2.0 copy-start
  130.1 5.0 %copy-start.22 = (bf16[1,128,960]{1,2,0:T(8,128)(2,1)S(1)}, bf16[1,128,960]{1,2,0:T(8,128)(2,1)}, u32[]{:S(2)}) copy-start(bf16[1,128,960]{1,2,0:T(8,128)(2,1)} %param.12) | copy-start | bytes 737284
  130.1 15.5 %slice-start.2 = ((s8[5242880]{0:T(1024)(128)(4,1)}), s8[1048576]{0:T(1024)(128)(4,1)S(1)}, s32[]{:S(2)}) async-start(s8[5242880]{0:T(1024)(128)(4,1)} %bitcast.146), calls=%async_computation.2 | async-start | bytes 2097152
  135.1 10.5 %slice-start.3 = ((s8[5242880]{0:T(1024)(128)(4,1)}), s8[4194304]{0:T(1024)(128)(4,1)S(1)}, s32[]{:S(2)}) async-start(s8[5242880]{0:T(1024)(128)(4,1)} %bitcast.146), calls=%async_computation.3 | async-start | bytes 8388608
  140.8 4.8 %copy-start.5 = (bf16[128,2560]{1,0:T(8,128)(2,1)}, bf16[128,2560]{1,0:T(8,128)(2,1)S(1)}, u32[]{:S(2)}) copy-start(bf16[128,2560]{1,0:T(8,128)(2,1)S(1)} %get-tuple-element.58.refs_1_) | copy-start | bytes 1966084
  140.8 4.8 %copy-start.4 = (bf16[128,2560]{1,0:T(8,128)(2,1)}, bf16[128,2560]{1,0:T(8,128)(2,1)S(1)}, u32[]{:S(2)}) copy-start(bf16[128,2560]{1,0:T(8,128)(2,1)S(1)} %get-tuple-element.57.refs_3_) | copy-start | bytes 1966084
  145.6 1.9 copy-start.47
  147.4 1.2 copy-start.36
  147.5 1.2 copy-start.44
  150.2 4.2 %copy-start.1 = (bf16[1,128,960]{2,1,0:T(8,128)(2,1)}, bf16[1,128,960]{2,1,0:T(8,128)(2,1)S(1)}, u32[]{:S(2)}) copy-start(bf16[1,128,960]{2,1,0:T(8,128)(2,1)S(1)} %copy.62) | copy-start | bytes 737284
  151.2 3.2 %copy-start.8 = (bf16[128,960]{1,0:T(8,128)(2,1)}, bf16[128,960]{1,0:T(8,128)(2,1)S(1)}, u32[]{:S(2)}) copy-start(bf16[128,960]{1,0:T(8,128)(2,1)S(1)} %fusion.99.refs_9_) | copy-start | bytes 737284
  154.4 1.3 copy-start.32
  155.7 0.8 copy-start.24
  155.7 0.8 copy-start.26
  155.7 1.0 copy-start.16
  155.7 1.0 copy-start.30
  156.5 0.9 copy-start.12
  156.5 1.0 copy-start.14
  156.7 1.1 copy-start.17
  159.3 3.4 %copy-start.6 = (bf16[128,1600]{1,0:T(8,128)(2,1)}, bf16[128,1600]{1,0:T(8,128)(2,1)S(1)}, u32[]{:S(2)}) copy-start(bf16[128,1600]{1,0:T(8,128)(2,1)S(1)} %concatenate.52) | copy-start | bytes 1228804
  159.3 3.4 %copy-start.48 = (s32[960]{0:T(1024)S(1)}, s32[960]{0:T(1024)}, u32[]{:S(2)}) copy-start(s32[960]{0:T(1024)} %copy-done.46) | copy-start | bytes 11524
  162.8 1.2 copy-start.40
  162.8 1.2 copy-start.50
  164.0 1.0 copy-start.2
  164.0 0.9 copy-start.37
  164.0 0.9 copy-start.45
  164.0 0.9 copy-start.51
  169.7 1.2 copy-start.7
  169.7 2.0 copy-start.41
  289.7 5.0 %copy-start.20 = (f32[32,2560]{1,0:T(8,128)S(1)}, f32[32,2560]{1,0:T(8,128)}, u32[]{:S(2)}) copy-start(f32[32,2560]{1,0:T(8,128)} %get-tuple-element.25) | copy-start | bytes 983044
  289.8 5.7 %copy-start.19 = (f32[32,2560]{1,0:T(8,128)S(1)}, f32[32,2560]{1,0:T(8,128)}, u32[]{:S(2)}) copy-start(f32[32,2560]{1,0:T(8,128)} %get-tuple-element.26) | copy-start | bytes 983044
  289.8 6.5 %copy-start.18 = (f32[80,960]{1,0:T(8,128)S(1)}, f32[80,960]{1,0:T(8,128)}, u32[]{:S(2)}) copy-start(f32[80,960]{1,0:T(8,128)} %get-tuple-element.27) | copy-start | bytes 921604
  289.8 7.4 %copy-start.42 = (f32[16,128]{1,0:T(8,128)S(1)}, f32[16,128]{1,0:T(8,128)}, u32[]{:S(2)}) copy-start(f32[16,128]{1,0:T(8,128)} %get-tuple-element.28) | copy-start | bytes 24580

commit v3 on v2

--- a/solution.py
+++ b/solution.py
@@ -462,29 +462,29 @@
     over_y = unit_index(z, 1 - y, x, c)
     meet(partners(me))
 
-    def build(a):
-        rows = grads[a].shape[4]
-
-        @pl.loop(0, PLANES)
-        def _(zz):
-            for left, right, at in factors[a]:
-                part = left[pl.ds(pl.multiple_of(zz * (8 * rows), 8 * rows), 8 * rows), :]
-                for start, width in column_tiles(right.shape[1], 512):
-                    value = jnp.dot(
-                        part, right[:, start : start + width], preferred_element_type=jnp.float32
-                    )
-                    grads[a][zz, :, :, :, :, at + start : at + start + width] = value.astype(
-                        grads[a].dtype
-                    ).reshape(2, 2, 2, rows, width)
-
     def plane(k):
         return (z + k) % PLANES
 
+    def build(a, k):
+        rows = grads[a].shape[4]
+        zz = plane(k)
+        for left, right, at in factors[a]:
+            part = left[pl.ds(pl.multiple_of(zz * (8 * rows), 8 * rows), 8 * rows), :]
+            for start, width in column_tiles(right.shape[1], 512):
+                value = jnp.dot(
+                    part, right[:, start : start + width], preferred_element_type=jnp.float32
+                )
+                grads[a][zz, :, :, :, :, at + start : at + start + width] = value.astype(
+                    grads[a].dtype
+                ).reshape(2, 2, 2, rows, width)
+        across(a, k).start()
+
     def copy(a, slot, source, target, device):
         return remote(source, target, send.at[a, slot], receive.at[a, slot], device)
 
-    def across(a):
-        return copy(a, 0, grads[a].at[:, :, :, 1 - c], sibling[a], over_core)
+    def across(a, k):
+        zz = plane(k)
+        return copy(a, 12 + k, grads[a].at[zz, :, :, 1 - c], sibling[a].at[zz], over_core)
 
     def first(a, k):
         zz = plane(k)
@@ -508,12 +508,13 @@
             target.dtype
         )
 
-    def fold_core(a):
-        across(a).wait_recv()
-
-        @pl.loop(0, PLANES * 4)
+    def fold_core(a, k):
+        across(a, k).wait_recv()
+        zz = plane(k)
+
+        @pl.loop(0, 4)
         def _(i):
-            zz, yy, xx = i // 4, (i // 2) % 2, i % 2
+            yy, xx = i // 2, i % 2
             add(grads[a].at[zz, yy, xx, c], sibling[a].at[zz, yy, xx])
 
     def fold_first(a, k):
@@ -568,27 +569,22 @@
     items = [
         (a, k) for pair in range(0, count, 2) for k in (1, 2, 3, 0) for a in (pair, pair + 1)
     ]
-    window = 4
-    folded = set()
-
-    def release(item):
-        if item[0] not in folded:
-            fold_core(item[0])
-            folded.add(item[0])
-        first(*item).start()
-
-    for a in range(2):
-        build(a)
-        across(a).start()
-    for item in items[:window]:
-        release(item)
-    for a in range(2, count):
-        build(a)
-        across(a).start()
+    window, ahead = 5, 3
+
+    def release(i):
+        fold_core(*items[i])
+        first(*items[i]).start()
+        if i + ahead < len(items):
+            build(*items[i + ahead])
+
+    for item in items[:ahead]:
+        build(*item)
+    for i in range(window):
+        release(i)
     for i, item in enumerate(items):
         fold_first(*item)
         if i + window < len(items):
-            release(items[i + window])
+            release(i + window)
         if i >= 2:
             fold_after(*items[i - 2])
         if i % 3 == 2 and i // 3 < 4:
@@ -602,8 +598,8 @@
             total = total + last[a][k - 1].astype(jnp.float32)
         outs[a][...] = total
     for a in range(count):
-        across(a).wait_send()
         for k in range(PLANES):
+            across(a, k).wait_send()
             first(a, k).wait_send()
             after(a, k).wait_send()
             if k > 0:
@@ -645,8 +641,8 @@
             pltpu.VMEM((2,) + gain.shape, gain.dtype),
             pltpu.VMEM(gain.shape, gain.dtype),
             pltpu.VMEM((PLANES,) + gain.shape, gain.dtype),
-            pltpu.SemaphoreType.DMA((count + 1, 12)),
-            pltpu.SemaphoreType.DMA((count + 1, 12)),
+            pltpu.SemaphoreType.DMA((count + 1, 16)),
+            pltpu.SemaphoreType.DMA((count + 1, 16)),
         ],
         compiler_params=pltpu.CompilerParams(
             collective_id=identity, has_side_effects=True, vmem_limit_bytes=56 * 1024 * 1024

time: 299 us -> 291 us (0.973)
  Pallas kernels: 225 us -> 218 us
    pallas_call x1, Pallas kernels: 117 us -> 110 us  [scatter_products(): pl.pallas_call(functools.partial(scatter_kernel, tuple(plan)), out_shape=...]
where the time goes in v3:
time: 291 us; the launch traced here: 290 us
  Pallas kernels  218 us (75%)
  matrix products  40.7 us (14%)
  local copies, waits for them, and re-layouts  23.1 us (8%)
  other arithmetic  7.3 us (3%)
    pallas_call x1, Pallas kernels, scatter_products(): pl.pallas_call(functools.partial(scatter_kernel, tuple(plan)), out_shape=...  110 us
    pallas_call x1, Pallas kernels, gather_blocks(): pl.pallas_call(functools.partial(gather_kernel, count), out_shape=[jax.Sh...  108 us
    dot_general x7, matrix products, back_product(): jnp.einsum('tf,df->td', left, right, preferred_element_type=jnp.float32)  21.2 us
    dot_general x8, matrix products, matrix_product(): return jnp.dot(left, right, preferred_element_type=jnp.float32)  16.8 us
    unnamed x124, local copies, waits for them, and re-layouts  6.42 us

profile of v3, /device:TPU:0, one launch (start us, length us, event | category | flops | bytes accessed | tf_op | source)
XLA Modules:
  0.0 290.5 jit_solution(278277209088788198)
XLA Ops:
  0.7 1.1 copy.55
  2.0 2.2 fusion.34
  4.8 0.7 pad.24.refs_0_
  5.5 0.2 reshape.327
  5.7 0.7 pad.25.refs_1_
  6.4 0.2 reshape.328
  6.6 0.7 pad.26.refs_2_
  7.3 0.8 reshape.329.refs_3_
  8.1 107.6 %shard_map.194 = (bf16[4,2,2,2,32,2624]{5,4,3,2,1,0:T(8,128)(2,1)}, bf16[4,2,2,2,32,2560]{5,4,3,2,1,0:T(8,128)(2,1)}, bf16[4,2,2,2,32,2560]{5,4,3,2,1,0:T(8,128)(2,1)}, bf16[4,2,2,2,80,960]{5,4,3,2,1,0:T(8,128)(2,1)}) custom-call(bf16[32,2624]{1,0:T(8,128)(2,1)} %pad.24.refs_0_, bf16[32,2560]{1,0:T(8,128)(2,1)} %pad.25.refs_1_, ...), custom_call_target="tpu_custom_call" | custom-call | tf_op jit(solution)/shard_map/pallas_call | solution.py:428
  115.7 3.5 %fusion.8 = f32[128,1600]{0,1:T(8,128)S(1)} fusion(bf16[128,1024]{0,1:T(8,128)(2,1)S(1)} %fusion.34, bf16[1024,2624]{1,0:T(8,128)(2,1)} %bitcast.162), kind=kOutput, calls=%fused_computation.10 | convolution fusion | flops 419430400 | bytes 4489216 | tf_op jit(solution)/shard_map/dot_general | solution.py:54
  119.3 0.8 broadcast_multiply_fusion
  120.3 0.4 fusion.105
  120.7 0.2 exponential_reduce_fusion
  120.9 0.6 copy-done.31
  121.5 0.1 exponential_convert_fusion
  121.6 0.2 convolution_convert_fusion
  121.9 1.4 fusion.35
  123.3 2.2 multiply_reduce_fusion.2
  125.6 1.4 fusion.36
  127.2 0.9 fusion.107
  128.1 2.0 fusion.106
  130.1 3.2 %fusion.38 = bf16[1,128,960]{2,1,0:T(8,128)(2,1)} fusion(f32[128,960]{1,0:T(8,128)S(1)} %get-tuple-element.85, bf16[2560,960]{1,0:T(8,128)(2,1)S(1)} %bitcast.183, f32[128,2560]{1,0:T(8,128)S(1)} %fusion.107, f32[128,2560]{1,0:T(8,128)} %fusion.106), kind=kOutput, calls=%fused_computation.50 | convolution fusion | flops 631357440 | bytes 8273920 | tf_op jit(solution)/shard_map/dot_general | solution.py:54
  133.3 1.8 copy.78
  135.1 5.7 %multiply_convert_fusion = (bf16[128,2560]{1,0:T(8,128)(2,1)S(1)}, bf16[128,2560]{1,0:T(8,128)(2,1)S(1)}) fusion(f32[128,2560]{1,0:T(8,128)} %fusion.106, f32[128,2560]{1,0:T(8,128)} %copy-done, bf16[2560,960]{1,0:T(8,128)(2,1)} %bitcast.180, bf16[1,128,960]{1,2,0:T(8,128)(2,1)S(1)} %copy-done.22), kind=kOutput, calls=%fused_computation.32 | convolution fusion | flops 633405440 | bytes 9093120 | tf_op jit(solution)/shard_map/tf,df->td/dot_general | solution.py:58
  140.8 4.7 %fusion.108 = f32[128,1024]{1,0:T(8,128)S(1)} fusion(bf16[128,2560]{1,0:T(8,128)(2,1)S(1)} %get-tuple-element.58.refs_1_, bf16[1024,2560]{1,0:T(8,128)(2,1)} %bitcast.149), kind=kOutput, calls=%fused_computation.165 | convolution fusion | flops 671088640 | bytes 6422528 | tf_op jit(solution)/shard_map/tf,df->td/dot_general | solution.py:58
  145.6 1.8 reduce-precision_convert_fusion.3
  147.5 1.2 fusion.2
  148.7 0.8 multiply_reduce_fusion
  149.5 0.6 broadcast_multiply_fusion.2
  150.1 0.1 copy.62
  150.2 0.9 fusion.99.refs_9_
  151.2 3.2 %fusion.37 = bf16[128,960]{0,1:T(8,128)(2,1)S(1)} fusion(s32[960]{0:T(1024)} %copy-done.46, bf16[128,960]{1,0:T(8,128)(2,1)S(1)} %fusion.99.refs_9_, bf16[1024,2624]{1,0:T(8,128)(2,1)} %bitcast.164), kind=kOutput, calls=%fused_computation.48 | convolution fusion | flops 504553472 | bytes 2592768 | tf_op jit(solution)/shard_map/tf,df->td/dot_general | solution.py:58
  154.5 1.2 fusion.42
  155.8 0.2 fusion.71
  156.0 0.5 copy-done.24
  156.5 0.2 fusion.82
  156.9 0.1 copy.70
  157.0 0.4 copy-done.12
  157.5 0.3 convolution_bitcast_fusion.3
  157.8 0.7 subtract_convert_fusion.2
  158.7 0.3 fusion.41
  159.2 0.1 concatenate.52
  159.4 3.4 %reduce-precision_convert_fusion.1 = (bf16[128,1024]{1,0:T(8,128)(2,1)S(1)}, bf16[128,1024]{1,0:T(8,128)(2,1)S(1)}, bf16[128,1024]{1,0:T(8,128)(2,1)S(1)}) fusion(bf16[128,1600]{1,0:T(8,128)(2,1)S(1)} %concatenate.52, bf16[1024,2624]{1,0:T(8,128)(2,1)} %bitcast.165), kind=kOutput, calls=%fused_computation.78 | convolution fusion | flops 420347904 | bytes 4603904 | tf_op jit(solution)/shard_map/tf,df->td/dot_general | solution.py:58
  162.8 1.2 fusion
  164.0 0.3 fusion.67
  164.4 0.6 copy-done.2
  165.0 0.3 fusion.66
  165.3 1.0 copy.79
  166.2 1.7 copy.77
  168.0 1.7 copy.76
  169.7 1.2 fusion.21.refs_4_
  170.9 0.8 pad.27.refs_7_
  171.7 0.7 fusion.83.refs_10_
  172.4 110.0 %shard_map.195 = (f32[32,2560]{1,0:T(8,128)}, f32[32,2560]{1,0:T(8,128)}, f32[80,960]{1,0:T(8,128)}, f32[32,2624]{1,0:T(8,128)}, f32[16,128]{1,0:T(8,128)}) custom-call(bf16[1024,128]{1,0:T(8,128)(2,1)} %bitcast.154, bf16[128,2560]{1,0:T(8,128)(2,1)} %copy-done.5, bf16[1024,128]{1,0:T(8,128)(2,1)} %bitcast.155, bf16[128,2560]{1,0:T(8,128)(2,1)} %copy-done.4, ...), custom_call_target="tpu_custom_call" | custom-call | tf_op jit(solution)/shard_map/pallas_call | solution.py:628
  282.5 1.1 fusion.102
  283.5 0.7 reshape.350
  284.3 1.0 fusion.103
  285.3 0.7 reshape.351
  286.0 0.7 reshape.352
  286.7 0.7 reshape.353
  287.4 0.7 reshape.354
  288.2 0.7 reshape.355
  288.9 0.9 reshape.356
  289.8 0.7 fusion.104
  (145 shorter events, 1.7 us)
Async XLA Ops:
  0.6 3.6 %copy-start.33 = (bf16[28800]{0:T(1024)(128)(2,1)S(1)}, bf16[28800]{0:T(1024)(128)(2,1)}, u32[]{:S(2)}) copy-start(bf16[28800]{0:T(1024)(128)(2,1)} %param.15) | copy-start | bytes 172804
  0.7 124.9 %copy-start.46 = (s32[960]{0:T(1024)}, s32[960]{0:T(1024)S(1)}, u32[]{:S(2)}) copy-start(s32[960]{0:T(1024)S(1)} %fusion.91) | copy-start | bytes 11524
  0.7 3.7 %copy-start.38 = (bf16[9600]{0:T(1024)(128)(2,1)S(1)}, bf16[9600]{0:T(1024)(128)(2,1)}, u32[]{:S(2)}) copy-start(bf16[9600]{0:T(1024)(128)(2,1)} %param.16) | copy-start | bytes 57604
  0.7 3.8 %copy-start.39 = (bf16[9600]{0:T(1024)(128)(2,1)S(1)}, bf16[9600]{0:T(1024)(128)(2,1)}, u32[]{:S(2)}) copy-start(bf16[9600]{0:T(1024)(128)(2,1)} %param.17) | copy-start | bytes 57604
  0.7 3.9 %copy-start.34 = (bf16[28800]{0:T(1024)(128)(2,1)S(1)}, bf16[28800]{0:T(1024)(128)(2,1)}, u32[]{:S(2)}) copy-start(bf16[28800]{0:T(1024)(128)(2,1)} %param.18) | copy-start | bytes 172804
  2.0 2.6 copy-start.49
  2.0 3.5 %copy-start.27 = (bf16[76800]{0:T(1024)(128)(2,1)S(1)}, bf16[76800]{0:T(1024)(128)(2,1)}, u32[]{:S(2)}) copy-start(bf16[76800]{0:T(1024)(128)(2,1)} %param.19) | copy-start | bytes 460804
  2.0 4.4 %copy-start.28 = (bf16[76800]{0:T(1024)(128)(2,1)S(1)}, bf16[76800]{0:T(1024)(128)(2,1)}, u32[]{:S(2)}) copy-start(bf16[76800]{0:T(1024)(128)(2,1)} %param.20) | copy-start | bytes 460804
  4.2 111.5 %copy-start.21 = (bf16[128,1024]{0,1:T(8,128)(2,1)}, bf16[128,1024]{0,1:T(8,128)(2,1)S(1)}, u32[]{:S(2)}) copy-start(bf16[128,1024]{0,1:T(8,128)(2,1)S(1)} %fusion.34) | copy-start | bytes 786436
  4.2 3.1 %copy-start.29 = (bf16[76800]{0:T(1024)(128)(2,1)S(1)}, bf16[76800]{0:T(1024)(128)(2,1)}, u32[]{:S(2)}) copy-start(bf16[76800]{0:T(1024)(128)(2,1)} %param.21) | copy-start | bytes 460804
  115.7 11.4 %slice-start = ((s8[5242880]{0:T(1024)(128)(4,1)}), s8[1048576]{0:T(1024)(128)(4,1)S(1)}, s32[]{:S(2)}) async-start(s8[5242880]{0:T(1024)(128)(4,1)} %bitcast.143), calls=%async_computation | async-start | bytes 2097152
  119.2 2.4 copy-start.10
  120.1 0.7 copy-start.15
  120.2 0.7 copy-start.11
  120.2 0.7 copy-start.13
  120.2 0.6 copy-start.23
  120.2 0.6 copy-start.25
  120.6 6.5 %slice-start.1 = ((s8[5242880]{0:T(1024)(128)(4,1)}), s8[4194304]{0:T(1024)(128)(4,1)S(1)}, s32[]{:S(2)}) async-start(s8[5242880]{0:T(1024)(128)(4,1)} %bitcast.143), calls=%async_computation.1 | async-start | bytes 8388608
  120.9 0.6 copy-start.31
  121.9 6.2 %slice-start.4 = ((s8[5242880]{0:T(1024)(128)(4,1)}), s8[4194304]{0:T(1024)(128)(4,1)S(1)}, s32[]{:S(2)}) async-start(s8[5242880]{0:T(1024)(128)(4,1)} %bitcast.150), calls=%async_computation.4 | async-start | bytes 8388608
  123.3 2.3 copy-start.9
  123.3 2.3 copy-start.35
  125.6 1.5 copy-start.43
  125.6 2.5 slice-start.5
  125.6 4.4 %slice-start.6 = ((s8[5242880]{0:T(1024)(128)(4,1)}), s8[4194304]{0:T(1024)(128)(4,1)S(1)}, s32[]{:S(2)}) async-start(s8[5242880]{0:T(1024)(128)(4,1)} %bitcast.181), calls=%async_computation.6 | async-start | bytes 8388608
  127.1 1.0 copy-start.3
  127.1 2.9 %slice-start.7 = ((s8[5242880]{0:T(1024)(128)(4,1)}), s8[1048576]{0:T(1024)(128)(4,1)S(1)}, s32[]{:S(2)}) async-start(s8[5242880]{0:T(1024)(128)(4,1)} %bitcast.181), calls=%async_computation.7 | async-start | bytes 2097152
  128.0 2.0 copy-start
  130.1 5.0 %copy-start.22 = (bf16[1,128,960]{1,2,0:T(8,128)(2,1)S(1)}, bf16[1,128,960]{1,2,0:T(8,128)(2,1)}, u32[]{:S(2)}) copy-start(bf16[1,128,960]{1,2,0:T(8,128)(2,1)} %param.12) | copy-start | bytes 737284
  130.1 15.5 %slice-start.2 = ((s8[5242880]{0:T(1024)(128)(4,1)}), s8[1048576]{0:T(1024)(128)(4,1)S(1)}, s32[]{:S(2)}) async-start(s8[5242880]{0:T(1024)(128)(4,1)} %bitcast.146), calls=%async_computation.2 | async-start | bytes 2097152
  135.1 10.5 %slice-start.3 = ((s8[5242880]{0:T(1024)(128)(4,1)}), s8[4194304]{0:T(1024)(128)(4,1)S(1)}, s32[]{:S(2)}) async-start(s8[5242880]{0:T(1024)(128)(4,1)} %bitcast.146), calls=%async_computation.3 | async-start | bytes 8388608
  140.8 4.8 %copy-start.5 = (bf16[128,2560]{1,0:T(8,128)(2,1)}, bf16[128,2560]{1,0:T(8,128)(2,1)S(1)}, u32[]{:S(2)}) copy-start(bf16[128,2560]{1,0:T(8,128)(2,1)S(1)} %get-tuple-element.58.refs_1_) | copy-start | bytes 1966084
  140.8 4.8 %copy-start.4 = (bf16[128,2560]{1,0:T(8,128)(2,1)}, bf16[128,2560]{1,0:T(8,128)(2,1)S(1)}, u32[]{:S(2)}) copy-start(bf16[128,2560]{1,0:T(8,128)(2,1)S(1)} %get-tuple-element.57.refs_3_) | copy-start | bytes 1966084
  145.6 1.9 copy-start.47
  147.4 1.2 copy-start.36
  147.5 1.2 copy-start.44
  150.2 4.2 %copy-start.1 = (bf16[1,128,960]{2,1,0:T(8,128)(2,1)}, bf16[1,128,960]{2,1,0:T(8,128)(2,1)S(1)}, u32[]{:S(2)}) copy-start(bf16[1,128,960]{2,1,0:T(8,128)(2,1)S(1)} %copy.62) | copy-start | bytes 737284
  151.2 3.2 %copy-start.8 = (bf16[128,960]{1,0:T(8,128)(2,1)}, bf16[128,960]{1,0:T(8,128)(2,1)S(1)}, u32[]{:S(2)}) copy-start(bf16[128,960]{1,0:T(8,128)(2,1)S(1)} %fusion.99.refs_9_) | copy-start | bytes 737284
  154.4 1.3 copy-start.32
  155.7 0.8 copy-start.24
  155.7 0.8 copy-start.26
  155.7 1.0 copy-start.16
  155.7 1.0 copy-start.30
  156.5 0.9 copy-start.12
  156.5 1.0 copy-start.14
  156.7 1.1 copy-start.17
  159.3 3.4 %copy-start.6 = (bf16[128,1600]{1,0:T(8,128)(2,1)}, bf16[128,1600]{1,0:T(8,128)(2,1)S(1)}, u32[]{:S(2)}) copy-start(bf16[128,1600]{1,0:T(8,128)(2,1)S(1)} %concatenate.52) | copy-start | bytes 1228804
  159.3 3.4 %copy-start.48 = (s32[960]{0:T(1024)S(1)}, s32[960]{0:T(1024)}, u32[]{:S(2)}) copy-start(s32[960]{0:T(1024)} %copy-done.46) | copy-start | bytes 11524
  162.8 1.2 copy-start.40
  162.8 1.2 copy-start.50
  164.0 1.0 copy-start.2
  164.0 0.9 copy-start.37
  164.0 0.9 copy-start.45
  164.0 0.9 copy-start.51
  169.7 1.2 copy-start.7
  169.7 2.0 copy-start.41
  282.4 5.0 %copy-start.20 = (f32[32,2560]{1,0:T(8,128)S(1)}, f32[32,2560]{1,0:T(8,128)}, u32[]{:S(2)}) copy-start(f32[32,2560]{1,0:T(8,128)} %get-tuple-element.25) | copy-start | bytes 983044
  282.4 5.7 %copy-start.19 = (f32[32,2560]{1,0:T(8,128)S(1)}, f32[32,2560]{1,0:T(8,128)}, u32[]{:S(2)}) copy-start(f32[32,2560]{1,0:T(8,128)} %get-tuple-element.26) | copy-start | bytes 983044
  282.4 6.5 %copy-start.18 = (f32[80,960]{1,0:T(8,128)S(1)}, f32[80,960]{1,0:T(8,128)}, u32[]{:S(2)}) copy-start(f32[80,960]{1,0:T(8,128)} %get-tuple-element.27) | copy-start | bytes 921604
  282.4 7.4 %copy-start.42 = (f32[16,128]{1,0:T(8,128)S(1)}, f32[16,128]{1,0:T(8,128)}, u32[]{:S(2)}) copy-start(f32[16,128]{1,0:T(8,128)} %get-tuple-element.28) | copy-start | bytes 24580
